TPU v7x, 32 devices: a whole 2x2x4 slice. The times are simulated.
32 devices in a mesh: seq: 8 (over y, x, core), tp: 4 (over z).
Axes of the slice: x: 2, y: 2, z: 4, core: 2. Of those that a mesh axis runs over, the one named last changes fastest.
Arguments:
- projected: bfloat16 [18560, 8192], P(('tp', 'seq')), may hold values from -4 to 53
- conv_weight: float32 [4, 8, 1280], P(None, 'tp'), may hold values from -3 to 3
- dt_bias: float32 [128], P('tp'), may hold values from -7 to -1
- a_log: float32 [128], P('tp'), may hold values from -7 to -1
- d_skip: float32 [128], P('tp'), may hold values from 0.5 to 2
- norm_gain: float32 [8192], P('tp'), may hold values from 0.25 to 1.75
Outputs:
- mixer_out: bfloat16 [8192, 8192], P('seq', 'tp')
All inputs are finite; a program needn't handle non-finite values.
Results may differ from a plain program's by a relative error of at most 0.0034.
Values may be sent and summed in bfloat16 or wider, within the bound.
No kernel may reach another device: no remote copies, remote signals or barrier semaphores. Data moves between devices by JAX's collectives and lax.ppermute only.
A program may use at most 192 MiB of HBM per device.

v0:
```python
import functools

import jax
import jax.numpy as jnp
from jax import lax
from jax.experimental import pallas as pl
from jax.experimental.pallas import tpu as pltpu
from jax.sharding import PartitionSpec as P

HEAD_DIM = 64
STATE_WIDTH = 128
BLOCK = 256
LANES = 128
HALF = BLOCK // 2
WIDE = 256
LOG2E = 1.4426950408889634
CAP = 80.0
EPSILON = 1e-05

f32 = jnp.float32
bf16 = jnp.bfloat16
NT = (((1,), (1,)), ((), ()))


def params(mib=60):
    return pltpu.CompilerParams(vmem_limit_bytes=mib * 2**20)


def silu(v):
    half = 0.5 * v
    return half + half * jnp.tanh(half)


def softplus(v):
    e = jnp.exp(-jnp.abs(v))
    u = 1.0 + e
    gap = u - 1.0
    tiny = gap == 0.0
    log_part = jnp.where(tiny, e, jnp.log(u) * (e / jnp.where(tiny, 1.0, gap)))
    return jnp.maximum(v, 0.0) + log_part


def in_hbm(*arrays):
    return [pltpu.with_memory_space_constraint(array, pltpu.HBM) for array in arrays]


def in_vmem(*arrays):
    return [pltpu.with_memory_space_constraint(array, pltpu.VMEM) for array in arrays]


def per_group(*shape):
    return pl.BlockSpec((1,) + shape, lambda g: (g,) + (0,) * len(shape))


RIM = 4


def rim_rows(rows, width):
    base = rows // 16 * 16
    height = -(-(rows - base + RIM * -(-rows // width)) // 8) * 8
    assert height <= 16
    return base, height


def first_kernel(src, dst, held, windows, ends, in_sems, rim_sems, out_sems, end_sems):
    rows, all_tokens = src.shape
    count, _, width = dst.shape
    tokens = all_tokens // count
    base, height = rim_rows(rows, width)

    def fetch(d):
        at = d * tokens
        return pltpu.make_async_copy(src.at[:, at : at + width], held.at[d], in_sems.at[d])

    def window(d):
        at = d * tokens - LANES
        return pltpu.make_async_copy(src.at[:, at : at + LANES], windows.at[d], rim_sems.at[d])

    def place(d):
        return pltpu.make_async_copy(
            held.at[d, :base, :], dst.at[d, :base, :], out_sems.at[d]
        )

    def place_end(d):
        return pltpu.make_async_copy(
            ends.at[d], dst.at[d, base : base + height, :], end_sems.at[d]
        )

    for d in range(count):
        fetch(d).start()
        if d:
            window(d).start()
    row = lax.broadcasted_iota(jnp.int32, (height, LANES), 0) - (rows - base)
    col = lax.broadcasted_iota(jnp.int32, (height, LANES), 1)
    hit = (row >= 0) & (col == lax.rem(row + 16, RIM) + LANES - RIM)
    pick = jnp.where(hit, 1.0, 0.0).astype(bf16)
    which = lax.broadcasted_iota(jnp.int32, (height, width), 0) - (rows - base)
    for d in range(count):
        fetch(d).wait()
        place(d).start()
        end = held[d, base:rows, :].astype(f32)
        end = jnp.concatenate([end, jnp.zeros((height - end.shape[0], width), f32)], axis=0)
        if d:
            window(d).wait()
            rims = lax.dot_general(pick, windows[d], NT, preferred_element_type=f32)
            for j in range(-(-rows // width)):
                part = rims[:, j * width : min((j + 1) * width, rows)]
                if part.shape[1] < width:
                    fill = jnp.zeros((height, width - part.shape[1]), f32)
                    part = jnp.concatenate([part, fill], axis=1)
                end = jnp.where((which >= RIM * j) & (which < RIM * (j + 1)), part, end)
        ends[d] = end.astype(bf16)
        place_end(d).start()
    for d in range(count):
        place(d).wait()
        place_end(d).wait()


def cut_first(projected, count, width):
    rows = projected.shape[0]
    base, height = rim_rows(rows, width)
    sems = pltpu.SemaphoreType.DMA((count,))
    anywhere = pl.BlockSpec(memory_space=pl.ANY)
    return pl.pallas_call(
        first_kernel,
        in_specs=[anywhere],
        out_specs=anywhere,
        out_shape=pltpu.HBM((count, base + height, width), bf16),
        scratch_shapes=[
            pltpu.VMEM((count, rows, width), bf16),
            pltpu.VMEM((count, rows, LANES), bf16),
            pltpu.VMEM((count, height, width), bf16),
            sems,
            sems,
            sems,
            sems,
        ],
        compiler_params=params(),
        name="cut_first",
    )(*in_hbm(projected))


def staged(moves, held, in_sems, out_sems):
    for i, (source, _) in enumerate(moves):
        pltpu.make_async_copy(source, held.at[i], in_sems.at[i]).start()
    for i, (source, target) in enumerate(moves):
        pltpu.make_async_copy(source, held.at[i], in_sems.at[i]).wait()
        pltpu.make_async_copy(held.at[i], target, out_sems.at[i]).start()
    for i, (_, target) in enumerate(moves):
        pltpu.make_async_copy(held.at[i], target, out_sems.at[i]).wait()


def staging(count, rows):
    sems = pltpu.SemaphoreType.DMA((count,))
    return [pltpu.VMEM((count, rows, BLOCK), bf16), sems, sems]


def cut_kernel(low, count, src, *refs):
    dst = refs[-4]
    tokens = src.shape[1] // count
    moves = []
    for d in range(count):
        at = d * tokens + low
        moves.append((src.at[:, at : at + BLOCK], dst.at[d]))
    staged(moves, *refs[-3:])


def cut_block(projected, count, low, after):
    rows = projected.shape[0]
    args = in_hbm(projected, *after)
    anywhere = pl.BlockSpec(memory_space=pl.ANY)
    return pl.pallas_call(
        functools.partial(cut_kernel, low, count),
        in_specs=[anywhere] * len(args),
        out_specs=anywhere,
        out_shape=pltpu.HBM((count, rows, BLOCK), bf16),
        scratch_shapes=staging(count, rows),
        compiler_params=params(),
        name="cut_block",
    )(*args)


def pairs_kernel(low, count, me_ref, src, *refs):
    own, near, *far = refs[-(count // 2 + 4) : -3]
    tokens = src.shape[1] // count
    me = me_ref[0]
    targets = [own, near]
    for pair in far:
        targets += [pair.at[:, :BLOCK], pair.at[:, BLOCK:]]
    moves = []
    for k, target in enumerate(targets):
        at = pl.multiple_of((me ^ k) * tokens + low, LANES)
        moves.append((src.at[:, pl.ds(at, BLOCK)], target))
    staged(moves[2:] + moves[:2], *refs[-3:])


def cut_pairs(projected, me, count, low, after):
    rows = projected.shape[0]
    anywhere = pl.BlockSpec(memory_space=pl.ANY)
    one, two = pltpu.HBM((rows, BLOCK), bf16), pltpu.HBM((rows, 2 * BLOCK), bf16)
    return pl.pallas_call(
        functools.partial(pairs_kernel, low, count),
        in_specs=[pl.BlockSpec(memory_space=pltpu.SMEM)] + [anywhere] * (1 + len(after)),
        out_specs=[anywhere] * (count // 2 + 1),
        out_shape=[one, one] + [two] * (count // 2 - 1),
        scratch_shapes=staging(count, rows),
        compiler_params=params(),
        name="cut_pairs",
    )(me, *in_hbm(projected, *after))


def forward_kernel(count, *refs):
    dst = refs[-4]
    moves = [
        (refs[j].at[:, BLOCK:], dst.at[:, j * BLOCK : (j + 1) * BLOCK])
        for j in range(count // 2 - 1)
    ]
    staged(moves, *refs[-3:])


def forward(pairs, after):
    count = 2 * len(pairs) + 2
    rows = pairs[0].shape[0]
    anywhere = pl.BlockSpec(memory_space=pl.ANY)
    return pl.pallas_call(
        functools.partial(forward_kernel, count),
        in_specs=[anywhere] * (len(pairs) + len(after)),
        out_specs=anywhere,
        out_shape=pltpu.HBM((rows, len(pairs) * BLOCK), bf16),
        scratch_shapes=staging(len(pairs), rows),
        compiler_params=params(),
        name="forward",
    )(*pairs, *in_hbm(*after))


def join_kernel(count, me_ref, own, near, *refs):
    others = count // 2 - 1
    pairs, passed, dst = refs[:others], refs[others], refs[-4]
    me = me_ref[0]
    sources = [own, near]
    for j in range(others):
        sources += [pairs[j].at[:, :BLOCK], passed.at[:, j * BLOCK : (j + 1) * BLOCK]]
    staged([(source, dst.at[me ^ k]) for k, source in enumerate(sources)], *refs[-3:])


def join(me, own, near, pairs, passed, after):
    count = 2 * len(pairs) + 2
    rows = own.shape[0]
    anywhere = pl.BlockSpec(memory_space=pl.ANY)
    args = [own, near, *pairs, passed, *in_hbm(*after)]
    return pl.pallas_call(
        functools.partial(join_kernel, count),
        in_specs=[pl.BlockSpec(memory_space=pltpu.SMEM)] + [anywhere] * len(args),
        out_specs=anywhere,
        out_shape=pltpu.HBM((count, rows, BLOCK), bf16),
        scratch_shapes=staging(count, rows),
        compiler_params=params(),
        name="join",
    )(me, *args)


def gather_rows(recv, prev, first, raw, rows, low, high, ahead=True, only=None):
    for s in range(recv.shape[0]):
        a = max(low - s * rows, 0) // 16 * 16
        b = min(-(-(high - s * rows) // 16) * 16, rows)
        if b <= a:
            continue
        at = s * rows + a
        raw[at : at + b - a, LANES:] = recv[s, a:b, :].astype(f32)
        if not ahead:
            continue
        if not first:
            raw[at : at + b - a, :LANES] = prev[s if only is None else 0, a:b, :].astype(f32)
            continue
        width = prev.shape[2]
        base, height = rim_rows(rows, width)
        rims = prev[s if only is None else 0, :height, :].astype(f32)
        tall = jnp.concatenate([jnp.zeros((LANES - height, width), f32), rims], axis=0)
        for j in range(-(-rows // width)):
            c, d = max(a, j * width), min(b, (j + 1) * width)
            if d <= c:
                continue
            shift = height - RIM - (rows - base) - RIM * j
            moved = (pltpu.roll(tall, shift, 0) if shift else tall).T
            raw[s * rows + c : s * rows + d, :LANES] = moved[c - j * width : d - j * width]


def band():
    row = lax.broadcasted_iota(jnp.int32, (2 * LANES, 3 * LANES), 0)
    col = lax.broadcasted_iota(jnp.int32, (2 * LANES, 3 * LANES), 1)
    tap = col // LANES
    return jnp.where(row == col - tap * LANES + LANES - 3 + tap, 1.0, 0.0).astype(bf16)


def shift_rows(raw, low, shifted, at):
    low[...] = raw[at : at + low.shape[0], :].astype(bf16)
    picks = band()
    for i in range(BLOCK // LANES):
        window = low[:, i * LANES : (i + 2) * LANES]
        shifted[i] = jnp.dot(window, picks, preferred_element_type=f32)


def conv_tile(raw, shifted, w, at, r):
    rows = slice(r, r + HEAD_DIM)
    taps = [jnp.broadcast_to(w[0, rows, k : k + 1], (HEAD_DIM, LANES)) for k in range(4)]
    parts = []
    for i in range(BLOCK // LANES):
        summed = None
        for k in range(3):
            part = taps[k] * shifted[i, rows, k * LANES : (k + 1) * LANES]
            summed = part if summed is None else summed + part
        own = raw[at + r : at + r + HEAD_DIM, (i + 1) * LANES : (i + 2) * LANES]
        parts.append(silu(summed + taps[3] * own).astype(bf16))
    return jnp.concatenate(parts, axis=1)


def state_kernel(dims, first, last, recv, *refs):
    spg, rows, heads, span, piece_heads = dims
    prev, refs = refs[0], refs[1:]
    w, bias, a_log, state_in, lead_in = refs[:5]
    xact, bmap, run_out, dt_out, cum_out, state_out, lead_out = refs[-11:-4]
    raw, xw, low, shifted = refs[-4:]
    steps = 2 * span + 2 * STATE_WIDTH

    gather_rows(recv, prev, first, raw, rows, steps, steps + heads, False)
    gather_rows(recv, prev, first, raw, rows, span, 2 * span + STATE_WIDTH)
    dt = softplus(raw[steps : steps + heads, LANES:] + bias[0])
    log_decay = -jnp.exp(a_log[0]) * dt
    lane = lax.broadcasted_iota(jnp.int32, (heads, BLOCK), 1)
    run = log_decay
    shift = 1
    while shift < BLOCK:
        run = run + jnp.where(lane >= shift, pltpu.roll(run, shift, 1), 0.0)
        shift *= 2
    final = run[:, BLOCK - 1 :]
    scale = jnp.exp(final - run) * dt
    cum = run + lead_in[0][:, :1]
    run_out[0] = run
    dt_out[0] = dt
    cum_out[0] = cum
    lead = jnp.broadcast_to(cum[:, BLOCK - 1 :], (heads, LANES))
    lead_out[0] = lead
    keep = jnp.broadcast_to(jnp.exp(final), (heads, LANES))

    shift_rows(raw, low, shifted, span)
    for r in range(0, STATE_WIDTH, HEAD_DIM):
        bmap[0, r : r + HEAD_DIM, :] = conv_tile(raw, shifted, w, span, span + r)
    for h in range(heads):
        r = h * HEAD_DIM
        tile = conv_tile(raw, shifted, w, span, r)
        xact[0, r : r + HEAD_DIM, :] = tile
        xw[r : r + HEAD_DIM, :] = (tile.astype(f32) * scale[h : h + 1, :]).astype(bf16)
    update = lax.dot_general(xw[...], bmap[0], NT, preferred_element_type=f32)
    for h in range(heads):
        r = h * HEAD_DIM
        new = update[r : r + HEAD_DIM, :]
        if not first:
            new = keep[h : h + 1, :] * state_in[0, r : r + HEAD_DIM, :] + new
        if last:
            at = (h % piece_heads) * HEAD_DIM
            state_out[h // piece_heads, at : at + HEAD_DIM, :] = new.astype(bf16)
        else:
            state_out[0, r : r + HEAD_DIM, :] = new
    if last:
        high, low = split(jnp.exp(lead))
        fill = jnp.zeros((8 - piece_heads, LANES), f32)
        for i in range(heads // piece_heads):
            mine = slice(i * piece_heads, (i + 1) * piece_heads)
            parts = [high[mine].astype(f32), fill, low[mine].astype(f32), fill]
            at = piece_heads * HEAD_DIM
            state_out[i, at : at + 16, :] = jnp.concatenate(parts, axis=0).astype(bf16)


def chunk_specs(got, chunk, dims, only=None):
    spg, rows = dims[:2]
    slabs = spg if only is None else 1

    def ahead(source, shape, row, lane):
        def index(g):
            return (g if only is None else g * spg + only, row, lane)

        return source, pl.BlockSpec((slabs,) + shape, index)

    def lane_of(block):
        first, middle, last = got
        ahead_of = first.shape[2] // BLOCK
        if block < ahead_of:
            return first, block
        return (middle if block == ahead_of else last), 0

    source, at = lane_of(chunk)
    block = pl.BlockSpec((spg, source.shape[1], BLOCK), lambda g: (g, 0, at))
    if chunk == 0:
        width = source.shape[2]
        prev, prev_spec = ahead(source, (16, width), rim_rows(rows, width)[0] // 16, 0)
    else:
        prev, place = lane_of(chunk - 1)
        lane = (place + 1) * (BLOCK // LANES) - 1
        prev, prev_spec = ahead(prev, (prev.shape[1], LANES), 0, lane)
    return [source, prev], [block, prev_spec]


def state_chunk(chunk, chunks, got, w, bias, a_log, state, lead, before, dims):
    spg, rows, heads, span, piece_heads = dims
    groups = w.shape[0]
    last = chunk == chunks - 1
    if last:
        packed = piece_heads * HEAD_DIM + 16
        state_shape = pltpu.HBM((groups * spg, packed, STATE_WIDTH), bf16)
        state_spec = pl.BlockSpec((spg, packed, STATE_WIDTH), lambda g: (g, 0, 0))
    else:
        state_shape = pltpu.HBM((groups, span, STATE_WIDTH), f32)
        state_spec = per_group(span, STATE_WIDTH)

    def out(dtype, *shape):
        return pltpu.HBM((groups,) + shape, dtype)

    args, specs = chunk_specs(got, chunk, dims)
    args[1:] = in_hbm(args[1])
    args[:1] = in_vmem(args[0]) if last else in_hbm(args[0])
    after = in_hbm(*before)
    return pl.pallas_call(
        functools.partial(state_kernel, dims, chunk == 0, last),
        grid=(groups,),
        in_specs=specs
        + [
            per_group(span + STATE_WIDTH, 4),
            per_group(heads, 1),
            per_group(heads, 1),
            per_group(span, STATE_WIDTH),
            per_group(heads, LANES),
        ]
        + [pl.BlockSpec(memory_space=pl.ANY)] * len(after),
        out_specs=[
            per_group(span, BLOCK),
            per_group(STATE_WIDTH, BLOCK),
            per_group(heads, BLOCK),
            per_group(heads, BLOCK),
            per_group(heads, BLOCK),
            state_spec,
            per_group(heads, LANES),
        ],
        out_shape=[
            out(bf16, span, BLOCK),
            out(bf16, STATE_WIDTH, BLOCK),
            out(f32, heads, BLOCK),
            out(f32, heads, BLOCK),
            out(f32, heads, BLOCK),
            state_shape,
            out(f32, heads, LANES),
        ],
        scratch_shapes=[
            pltpu.VMEM((rows * spg, LANES + BLOCK), f32),
            pltpu.VMEM((span, BLOCK), bf16),
            pltpu.VMEM((span + STATE_WIDTH, LANES + BLOCK), bf16),
            pltpu.VMEM((BLOCK // LANES, span + STATE_WIDTH, 3 * LANES), f32),
        ],
        compiler_params=params(48 if last else 60),
        cost_estimate=pl.CostEstimate(flops=4 * 10**9, bytes_accessed=10**7, transcendentals=10**6),
        name="state_chunk",
    )(*args, *in_hbm(w, bias, a_log, state, lead), *after)


def split(v):
    high = v.astype(bf16)
    return high, (v - high.astype(f32)).astype(bf16)


def block_kernel(dims, first, recv, *refs):
    spg, rows, heads, span, piece_heads = dims
    prev, refs = refs[0], refs[1:]
    w, xact, bmap, run_ref, dt_ref, cum_ref, state, skip = refs[:8]
    mixed, gate_out, side, token, raw, low, shifted = refs[-7:]
    at_c = 2 * span + STATE_WIDTH
    gather_rows(recv, prev, first, raw, rows, at_c, at_c + STATE_WIDTH, True, at_c // rows)
    gather_rows(recv, prev, first, raw, rows, 0, span, False)
    token[0] = cum_ref[0, :8, :LANES]
    shift_rows(raw, low, shifted, at_c)
    c = [conv_tile(raw, shifted, w, at_c, r) for r in range(0, STATE_WIDTH, HEAD_DIM)]
    c = jnp.concatenate(c, axis=0)
    b_rows = bmap[0].astype(f32).T.astype(bf16)
    scores = jnp.dot(b_rows, c, preferred_element_type=f32)
    src = lax.broadcasted_iota(jnp.int32, (HALF, HALF), 0)
    dst = lax.broadcasted_iota(jnp.int32, (HALF, HALF), 1)
    causal = src <= dst
    s00 = jnp.where(causal, scores[:HALF, :HALF], 0.0)
    s01 = scores[:HALF, HALF:]
    s11 = jnp.where(causal, scores[HALF:, HALF:], 0.0)
    r = run_ref[0] * LOG2E
    q = (r - jnp.log(dt_ref[0]) * LOG2E).T
    if not first:
        cc = jnp.concatenate([c, c], axis=0)
        entered = jnp.exp2(r)
    reach = [part.astype(f32) for part in split(jnp.exp(cum_ref[0]))]
    reach.append(jnp.zeros((STATE_WIDTH - 2 * heads, BLOCK), f32))
    side[0, :, :STATE_WIDTH] = c.astype(f32).T.astype(bf16)
    side[0, :, STATE_WIDTH:] = jnp.concatenate(reach, axis=0).T.astype(bf16)
    turned = []
    for h in range(heads):
        at = h * HEAD_DIM
        r0, r1 = r[h : h + 1, :HALF], r[h : h + 1, HALF:]
        q0, q1 = q[:HALF, h : h + 1], q[HALF:, h : h + 1]
        w00 = (s00 * jnp.exp2(jnp.minimum(r0 - q0, CAP))).astype(bf16)
        w01 = (s01 * jnp.exp2(r1 - q0)).astype(bf16)
        w11 = (s11 * jnp.exp2(jnp.minimum(r1 - q1, CAP))).astype(bf16)
        x = xact[0, at : at + HEAD_DIM, :]
        y0 = jnp.dot(x[:, :HALF], w00, preferred_element_type=f32)
        y1 = jnp.dot(x, jnp.concatenate([w01, w11], axis=0), preferred_element_type=f32)
        y = jnp.concatenate([y0, y1], axis=1) + skip[0, h : h + 1, :] * x.astype(f32)
        if not first:
            if at % WIDE == 0:
                both = jnp.concatenate(split(state[0, at : at + WIDE, :]), axis=1)
                carried = jnp.dot(both, cc, preferred_element_type=f32)
            y = y + entered[h : h + 1, :] * carried[at % WIDE : at % WIDE + HEAD_DIM, :]
        gate = raw[at : at + HEAD_DIM, LANES:]
        turned.append((y * silu(gate), gate))
        if len(turned) * HEAD_DIM == LANES:
            lanes = slice(at + HEAD_DIM - LANES, at + HEAD_DIM)
            mixed[0, :, lanes] = jnp.concatenate([pair[0] for pair in turned], axis=0).T
            wide = jnp.concatenate([pair[1] for pair in turned], axis=0).T
            gate_out[0, :, lanes] = wide.astype(bf16)
            turned = []


def block_chunk(
    chunk, chunks, got, w, xact, bmap, run, dt, cum, state, skip, after, dims
):
    spg, rows, heads, span, piece_heads = dims
    groups = w.shape[0]

    at_c = 2 * span + STATE_WIDTH
    one = at_c // rows
    assert (at_c + STATE_WIDTH - 1) // rows == one
    args, specs = chunk_specs(got, chunk, dims, one)
    args = in_hbm(*args)
    args += in_hbm(w, xact, bmap, run, dt, cum, state, skip)
    specs += [
        pl.BlockSpec((1, STATE_WIDTH, 4), lambda g: (g, span // STATE_WIDTH + 1, 0)),
        per_group(span, BLOCK),
        per_group(STATE_WIDTH, BLOCK),
        per_group(heads, BLOCK),
        per_group(heads, BLOCK),
        per_group(heads, BLOCK),
        per_group(span, STATE_WIDTH),
        per_group(heads, 1),
    ]
    args += in_vmem(*after)
    specs += [pl.BlockSpec(memory_space=pl.ANY)] * len(after)

    def out(dtype, *shape):
        return pltpu.HBM((groups,) + shape, dtype)

    return pl.pallas_call(
        functools.partial(block_kernel, dims, chunk == 0),
        grid=(groups,),
        in_specs=specs,
        out_specs=[
            per_group(BLOCK, span),
            per_group(BLOCK, span),
            per_group(BLOCK, 2 * STATE_WIDTH),
            per_group(8, LANES),
        ],
        out_shape=[
            out(f32, BLOCK, span),
            out(bf16, BLOCK, span),
            out(bf16, BLOCK, 2 * STATE_WIDTH),
            out(f32, 8, LANES),
        ],
        scratch_shapes=[
            pltpu.VMEM((rows * spg, LANES + BLOCK), f32),
            pltpu.VMEM((STATE_WIDTH, LANES + BLOCK), bf16),
            pltpu.VMEM((BLOCK // LANES, STATE_WIDTH, 3 * LANES), f32),
        ],
        compiler_params=params(),
        cost_estimate=pl.CostEstimate(flops=4 * 10**9, bytes_accessed=10**7, transcendentals=10**6),
        name="block_chunk",
    )(*args)


def relay_kernel(piece_heads, src, token, dst):
    rows = piece_heads * HEAD_DIM
    held = jnp.zeros((rows, STATE_WIDTH), f32)
    for d in range(src.shape[0]):
        dst[d] = held.T.astype(bf16)
        both = src[d, rows:, :].astype(f32)
        decay = both[:8] + both[8:]
        spread = [
            jnp.broadcast_to(decay[h : h + 1, :], (HEAD_DIM, STATE_WIDTH))
            for h in range(piece_heads)
        ]
        held = jnp.concatenate(spread, axis=0) * held + src[d, :rows, :].astype(f32)


def relay(packed, token, piece_heads):
    count = packed.shape[0]
    rows = piece_heads * HEAD_DIM
    return pl.pallas_call(
        functools.partial(relay_kernel, piece_heads),
        in_specs=[pl.BlockSpec(memory_space=pltpu.VMEM), pl.BlockSpec(memory_space=pl.ANY)],
        out_shape=pltpu.VMEM((count, STATE_WIDTH, rows), bf16),
        compiler_params=params(16),
        name="relay",
    )(packed, *in_hbm(token))


def final_kernel(chunks, groups, *refs):
    mixed, gates, sides = (refs[i * chunks : (i + 1) * chunks] for i in range(3))
    state, gain, out = refs[3 * chunks : 3 * chunks + 3]
    held, gate_held, side_held, kept, carried, done, sems, out_sems = refs[3 * chunks + 3 :]
    span = held.shape[2]
    piece = state.shape[2]
    spg = state.shape[0] // groups
    heads = span // HEAD_DIM
    steps = [(g, c) for g in range(groups) for c in range(chunks)]

    def loads(i):
        g, c = steps[i]
        slot = i
        moves = []
        moves.append((sides[c].at[g], side_held.at[slot]))
        moves.append((mixed[c].at[g], held.at[slot]))
        moves.append((gates[c].at[g], gate_held.at[slot]))
        return [
            pltpu.make_async_copy(a, b, sems.at[slot, j]) for j, (a, b) in enumerate(moves)
        ]

    def store(i):
        g, c = steps[i]
        return pltpu.make_async_copy(
            done.at[i % 2],
            out.at[c * BLOCK : (c + 1) * BLOCK, g * span : (g + 1) * span],
            out_sems.at[i % 2],
        )

    for i in range(len(steps)):
        for move in loads(i):
            move.start()
    row = lax.broadcasted_iota(jnp.int32, (STATE_WIDTH, span), 0)
    col = lax.broadcasted_iota(jnp.int32, (STATE_WIDTH, span), 1) // HEAD_DIM
    spread = jnp.where((row == col) | (row == col + heads), 1.0, 0.0).astype(bf16)
    for i, (g, c) in enumerate(steps):
        slot = i
        for move in loads(i):
            move.wait()
        if i >= 2:
            store(i - 2).wait()
        side = side_held[slot]
        reach = jnp.dot(side[:, STATE_WIDTH:], spread, preferred_element_type=f32)
        for j in range(spg):
            lanes = slice(j * piece, (j + 1) * piece)
            part = jnp.dot(
                side[:, :STATE_WIDTH], state[g * spg + j], preferred_element_type=f32
            )
            carried[:, lanes] = part * reach[:, lanes]
        for q in range(0, BLOCK, HEAD_DIM):
            rows = slice(q, q + HEAD_DIM)
            total = jnp.zeros((HEAD_DIM, LANES), f32)
            for at in range(0, span, LANES):
                lanes = slice(at, at + LANES)
                gate = silu(gate_held[slot, rows, lanes].astype(f32))
                v = held[slot, rows, lanes] + gate * carried[rows, lanes]
                kept[rows, lanes] = v
                total = total + v * v
            mean = jnp.sum(total, axis=1, keepdims=True) * (1.0 / span)
            factor = lax.rsqrt(mean + EPSILON)
            for at in range(0, span, LANES):
                lanes = slice(at, at + LANES)
                scaled = kept[rows, lanes] * factor * gain[g, :, lanes]
                done[i % 2, rows, lanes] = scaled.astype(bf16)
        store(i).start()
    for i in range(max(len(steps) - 2, 0), len(steps)):
        store(i).wait()


def finish(mixed, gates, sides, state, gain):
    chunks = len(mixed)
    groups, _, span = mixed[0].shape
    steps = groups * chunks
    anywhere = pl.BlockSpec(memory_space=pl.ANY)
    within = pl.BlockSpec(memory_space=pltpu.VMEM)
    return pl.pallas_call(
        functools.partial(final_kernel, chunks, groups),
        in_specs=[anywhere] * (3 * chunks) + [within] * 2,
        out_specs=anywhere,
        out_shape=jax.ShapeDtypeStruct((chunks * BLOCK, groups * span), bf16),
        scratch_shapes=[
            pltpu.VMEM((steps, BLOCK, span), f32),
            pltpu.VMEM((steps, BLOCK, span), bf16),
            pltpu.VMEM((steps, BLOCK, 2 * STATE_WIDTH), bf16),
            pltpu.VMEM((BLOCK, span), f32),
            pltpu.VMEM((BLOCK, span), f32),
            pltpu.VMEM((2, BLOCK, span), bf16),
            pltpu.SemaphoreType.DMA((steps, 3)),
            pltpu.SemaphoreType.DMA((2,)),
        ],
        compiler_params=params(40),
        name="finish",
    )(*in_hbm(*mixed, *gates, *sides), state, gain)


def swap(array, k):
    count = lax.axis_size("seq")
    return lax.ppermute(array, "seq", [(i, i ^ k) for i in range(count)])


def exchange(array):
    return lax.all_to_all(array, "seq", split_axis=0, concat_axis=0, tiled=True)


def per_device(projected, conv_weight, dt_bias, a_log, d_skip, norm_gain):
    seq_count = lax.axis_size("seq")
    groups = conv_weight.shape[1]
    heads = dt_bias.shape[0] // groups
    span = heads * HEAD_DIM
    rows, all_tokens = projected.shape
    local_tokens = all_tokens // seq_count
    chunks = local_tokens // BLOCK
    spg = seq_count // groups
    piece_heads = groups * heads // seq_count
    dims = (spg, rows, heads, span, piece_heads)

    w = jnp.transpose(conv_weight, (1, 2, 0))
    bias = dt_bias.reshape(groups, heads, 1)
    rate = a_log.reshape(groups, heads, 1)
    skip = d_skip.reshape(groups, heads, 1)
    gain = norm_gain.reshape(groups, 1, span)
    state = jnp.zeros((groups, span, STATE_WIDTH), f32)
    lead = jnp.zeros((groups, heads, LANES), f32)

    me = lax.axis_index("seq").astype(jnp.int32).reshape(1)
    assert chunks > 2 and seq_count & (seq_count - 1) == 0
    cut = cut_first(projected, seq_count, local_tokens - 2 * BLOCK)
    got = [exchange(cut)]
    own, near, *pairs = cut_pairs(projected, me, seq_count, local_tokens - 2 * BLOCK, [cut])
    near = swap(near, 1)
    pairs = [swap(pair, 2 * j + 2) for j, pair in enumerate(pairs)]
    ready = [own, w, bias, rate, skip, gain, state, lead]
    cut = cut_block(projected, seq_count, local_tokens - BLOCK, ready)
    got += [None, exchange(cut)]

    results, tokens = [], []
    for c in range(chunks):
        before = []
        if c == chunks - 2:
            passed = swap(forward(pairs, [lead, tokens[0]]), 1)
            got[1] = join(me, own, near, pairs, passed, tokens)
        if c == chunks - 1:
            before = tokens[-2:-1]
        xact, bmap, run, dt, cum, new, lead = state_chunk(
            c, chunks, got, w, bias, rate, state, lead, before, dims
        )
        after = []
        if c == chunks - 1:
            entering = relay(exchange(new), tokens[-1], piece_heads)
            after = [entering]
        *result, token = block_chunk(
            c, chunks, got, w, xact, bmap, run, dt, cum, state, skip, after, dims
        )
        results.append(result)
        tokens.append(token)
        state = new
    return finish(*zip(*results), exchange(entering), gain)


def solution(mesh):
    in_specs = (P(("tp", "seq"), None), P(None, "tp", None), P("tp"), P("tp"), P("tp"), P("tp"))
    return jax.shard_map(
        per_device, mesh=mesh, in_specs=in_specs, out_specs=P("seq", "tp"), check_vma=False
    )
```

profile of v0, /device:TPU:0, one launch (start us, length us, event | category | flops | bytes accessed | tf_op | source)
XLA Modules:
  0.0 160.6 jit_solution(13875208905295406601)
XLA Ops:
  0.0 5.1 %cut_first.1.refs_0_ = bf16[8,592,512]{2,1,0:T(8,128)(2,1)} custom-call(bf16[580,8192]{1,0:T(8,128)(2,1)} %src.5), custom_call_target="tpu_custom_call" | custom-call | tf_op jit(solution)/shard_map/cut_first/pallas_call | solution.py:124
  5.1 5.2 %all-to-all-start = ((bf16[8,592,512]{2,1,0:T(8,128)(2,1)}), bf16[8,592,512]{2,1,0:T(8,128)(2,1)}, u32[]{:S(2)}, u32[]{:S(2)}) async-start(bf16[8,592,512]{2,1,0:T(8,128)(2,1)} %cut_first.1.refs_0_), calls=%async_computation | async-start | bytes 9699328 | tf_op jit(solution)/shard_map/all_to_all | solution.py:707
  10.3 2.6 %cut_pairs.1 = (bf16[580,256]{1,0:T(8,128)(2,1)}, bf16[580,256]{1,0:T(8,128)(2,1)}, bf16[580,512]{1,0:T(8,128)(2,1)}, bf16[580,512]{1,0:T(8,128)(2,1)}, bf16[580,512]{1,0:T(8,128)(2,1)}) custom-call(s32[1]{0:T(128)} %bitcast.1.me_ref, bf16[580,8192]{1,0:T(8,128)(2,1)} %src.5, bf16[8,592,512]{2,1,0:T(8,128)(2,1)} %cut_first.1.refs_0_), custom_call_target="tpu_custom_call" | custom-call | tf_op jit(solution)/shard_map/cut_pairs/pallas_call | solution.py:201
  12.9 2.4 %collective-permute-start.1 = (bf16[580,512]{1,0:T(8,128)(2,1)}, bf16[580,512]{1,0:T(8,128)(2,1)S(1)}, u32[]{:S(2)}, u32[]{:S(2)}) collective-permute-start(bf16[580,512]{1,0:T(8,128)(2,1)} %get-tuple-element.68), channel_id=1, source_target_pairs={{0,8},{4,12},{8,0},{12,4},{16,24},{20,28},{24,16},{28,20},{1,9},{5... | collective-permute-start | bytes 1781768 | tf_op jit(solution)/shard_map/ppermute | solution.py:703
  15.3 1.5 collective-permute-start.2
  16.9 1.5 copy.7
  18.4 0.7 reshape.20.refs_2_
  19.1 0.7 reshape.21.refs_3_
  19.8 0.7 reshape.22.refs_8_.refs_4_
  20.5 1.0 broadcast_in_dim.6.refs_4_.refs_7_.refs_6_
  22.1 2.5 %cut_block.1 = bf16[8,580,256]{2,1,0:T(8,128)(2,1)} custom-call(bf16[580,8192]{1,0:T(8,128)(2,1)} %src.5, bf16[580,256]{1,0:T(8,128)(2,1)} %get-tuple-element.66.own.refs_0_, f32[2,1280,4]{2,1,0:T(8,128)} %bitcast.5, f32[2,16,1]{2,1,0:T(8,128)} %reshape.20.refs_2_, f32[2,16,1]{2,1,0:T(8,128)} %reshape.21.refs_3_, f32[2,16,1]{2,1,0:T(8,128)} %reshape.22.refs_8_.refs_4_, ...), custom_call_target="tpu_custom_call" | custom-call | tf_op jit(solution)/shard_map/cut_block/pallas_call | solution.py:172
  24.6 42.7 %all-to-all-done.recv.refs_0_ = bf16[8,592,512]{2,1,0:T(8,128)(2,1)} async-done(((bf16[8,592,512]{2,1,0:T(8,128)(2,1)}), bf16[8,592,512]{2,1,0:T(8,128)(2,1)}, u32[]{:S(2)}, u32[]{:S(2)}) %all-to-all-start) | async-done | bytes 4849696 | tf_op jit(solution)/shard_map/all_to_all | solution.py:707
  67.4 3.6 %all-to-all-start.1 = ((bf16[8,580,256]{2,1,0:T(8,128)(2,1)}), bf16[8,580,256]{2,1,0:T(8,128)(2,1)S(1)}, u32[]{:S(2)}, u32[]{:S(2)}) async-start(bf16[8,580,256]{2,1,0:T(8,128)(2,1)} %cut_block.1), calls=%async_computation.1 | async-start | bytes 4784128 | tf_op jit(solution)/shard_map/all_to_all | solution.py:707
  71.0 6.1 %state_chunk.4 = (bf16[2,1024,256]{2,1,0:T(8,128)(2,1)}, bf16[2,128,256]{2,1,0:T(8,128)(2,1)}, f32[2,16,256]{2,1,0:T(8,128)}, f32[2,16,256]{2,1,0:T(8,128)}, f32...) custom-call(bf16[8,592,512]{2,1,0:T(8,128)(2,1)} %all-to-all-done.recv.refs_0_, ...), custom_call_target="tpu_custom_call" | custom-call | flops 4000000000 | bytes 10000000 | tf_op jit(solution)/shard_map/state_chunk/pallas_call | solution.py:422
  77.1 6.0 %state_chunk.5 = (bf16[2,1024,256]{2,1,0:T(8,128)(2,1)}, bf16[2,128,256]{2,1,0:T(8,128)(2,1)}, f32[2,16,256]{2,1,0:T(8,128)}, f32[2,16,256]{2,1,0:T(8,128)}, f32...) custom-call(bf16[8,592,512]{2,1,0:T(8,128)(2,1)} %all-to-all-done.recv.refs_0_, ...), custom_call_target="tpu_custom_call" | custom-call | flops 4000000000 | bytes 10000000 | tf_op jit(solution)/shard_map/state_chunk/pallas_call | solution.py:422
  83.0 6.2 %block_chunk.4 = (f32[2,256,1024]{2,1,0:T(8,128)}, bf16[2,256,1024]{2,1,0:T(8,128)(2,1)}, bf16[2,256,256]{2,1,0:T(8,128)(2,1)}, f32[2,8,128]{2,1,0:T(8,128)}) custom-call(bf16[8,592,512]{2,1,0:T(8,128)(2,1)} %all-to-all-done.recv.refs_0_, bf16[8,592,512]{2,1,0:T(8,128)(2,1)} %all-to-all-done.recv.refs_0_, f32[2,1280,4]{2,1,0:T(8,128)} %bitcast.8, ...), custom_call_target="tpu_custom_call" | custom-call | flops 4000000000 | bytes 10000000 | tf_op jit(solution)/shard_map/block_chunk/pallas_call | solution.py:553
  89.3 3.7 %collective-permute-done.3.refs_2_ = bf16[580,512]{1,0:T(8,128)(2,1)} collective-permute-done((bf16[580,512]{1,0:T(8,128)(2,1)}, bf16[580,512]{1,0:T(8,128)(2,1)}, u32[]{:S(2)}, u32[]{:S(2)}) %collective-permute-start.3) | collective-permute-done | bytes 593952 | tf_op jit(solution)/shard_map/ppermute | solution.py:703
  93.0 1.9 %forward.1 = bf16[580,768]{1,0:T(8,128)(2,1)} custom-call(bf16[580,512]{1,0:T(8,128)(2,1)} %copy-done.2, bf16[580,512]{1,0:T(8,128)(2,1)} %collective-permute-done.2.refs_1_, bf16[580,512]{1,0:T(8,128)(2,1)} %collective-permute-done.3.refs_2_, f32[2,16,128]{2,1,0:T(8,128)} %get-tuple-element.71.refs_3_.refs_5_, f32[2,8,128]{2,1,0:T(8,128)} %get-tuple-element.72.refs_4_), custom_call_target="tpu_custom_call" | custom-call | tf_op jit(solution)/shard_map/forward/pallas_call | solution.py:225
  95.5 6.6 %block_chunk.5 = (f32[2,256,1024]{2,1,0:T(8,128)}, bf16[2,256,1024]{2,1,0:T(8,128)(2,1)}, bf16[2,256,256]{2,1,0:T(8,128)(2,1)}, f32[2,8,128]{2,1,0:T(8,128)}) custom-call(bf16[8,592,512]{2,1,0:T(8,128)(2,1)} %all-to-all-done.recv.refs_0_, bf16[8,592,512]{2,1,0:T(8,128)(2,1)} %all-to-all-done.recv.refs_0_, f32[2,1280,4]{2,1,0:T(8,128)} %bitcast.9, ...), custom_call_target="tpu_custom_call" | custom-call | flops 4000000000 | bytes 10000000 | tf_op jit(solution)/shard_map/block_chunk/pallas_call | solution.py:553
  102.2 0.7 copy-done.4
  103.2 2.5 %join.1.recv.refs_0_ = bf16[8,580,256]{2,1,0:T(8,128)(2,1)} custom-call(s32[1]{0:T(128)} %bitcast.1.me_ref, bf16[580,256]{1,0:T(8,128)(2,1)} %get-tuple-element.66.own.refs_0_, bf16[580,256]{1,0:T(8,128)(2,1)} %copy-done.4, bf16[580,512]{1,0:T(8,128)(2,1)} %copy-done.2, bf16[580,512]{1,0:T(8,128)(2,1)} %collective-permute-done.2.refs_1_, ...), custom_call_target="tpu_custom_call" | custom-call | tf_op jit(solution)/shard_map/join/pallas_call | solution.py:251
  105.8 6.0 %state_chunk.6 = (bf16[2,1024,256]{2,1,0:T(8,128)(2,1)}, bf16[2,128,256]{2,1,0:T(8,128)(2,1)}, f32[2,16,256]{2,1,0:T(8,128)}, f32[2,16,256]{2,1,0:T(8,128)}, f32...) custom-call(bf16[8,580,256]{2,1,0:T(8,128)(2,1)} %join.1.recv.refs_0_, ...), custom_call_target="tpu_custom_call" | custom-call | flops 4000000000 | bytes 10000000 | tf_op jit(solution)/shard_map/state_chunk/pallas_call | solution.py:422
  111.7 6.1 %all-to-all-done.1.recv = bf16[8,580,256]{2,1,0:T(8,128)(2,1)S(1)} async-done(((bf16[8,580,256]{2,1,0:T(8,128)(2,1)}), bf16[8,580,256]{2,1,0:T(8,128)(2,1)S(1)}, u32[]{:S(2)}, u32[]{:S(2)}) %all-to-all-start.1) | async-done | bytes 2375712 | tf_op jit(solution)/shard_map/all_to_all | solution.py:707
  117.8 6.4 %state_chunk.7 = (bf16[2,1024,256]{2,1,0:T(8,128)(2,1)}, bf16[2,128,256]{2,1,0:T(8,128)(2,1)}, f32[2,16,256]{2,1,0:T(8,128)}, f32[2,16,256]{2,1,0:T(8,128)}, f32...) custom-call(bf16[8,580,256]{2,1,0:T(8,128)(2,1)S(1)} %all-to-all-done.1.recv, ...), custom_call_target="tpu_custom_call" | custom-call | flops 4000000000 | bytes 10000000 | tf_op jit(solution)/shard_map/state_chunk/pallas_call | solution.py:422
  124.2 3.7 %all-to-all-start.2 = ((bf16[8,272,128]{2,1,0:T(8,128)(2,1)}), bf16[8,272,128]{2,1,0:T(8,128)(2,1)S(1)}, u32[]{:S(2)}, u32[]{:S(2)}) async-start(bf16[8,272,128]{2,1,0:T(8,128)(2,1)} %get-tuple-element.88), calls=%async_computation.2 | async-start | bytes 1114112 | tf_op jit(solution)/shard_map/all_to_all | solution.py:707
  127.9 6.6 %block_chunk.6 = (f32[2,256,1024]{2,1,0:T(8,128)}, bf16[2,256,1024]{2,1,0:T(8,128)(2,1)}, bf16[2,256,256]{2,1,0:T(8,128)(2,1)}, f32[2,8,128]{2,1,0:T(8,128)}) custom-call(bf16[8,580,256]{2,1,0:T(8,128)(2,1)} %join.1.recv.refs_0_, bf16[8,592,512]{2,1,0:T(8,128)(2,1)} %all-to-all-done.recv.refs_0_, f32[2,1280,4]{2,1,0:T(8,128)} %bitcast.12, ...), custom_call_target="tpu_custom_call" | custom-call | flops 4000000000 | bytes 10000000 | tf_op jit(solution)/shard_map/block_chunk/pallas_call | solution.py:553
  134.5 3.2 %all-to-all-done.2.src = bf16[8,272,128]{2,1,0:T(8,128)(2,1)S(1)} async-done(((bf16[8,272,128]{2,1,0:T(8,128)(2,1)}), bf16[8,272,128]{2,1,0:T(8,128)(2,1)S(1)}, u32[]{:S(2)}, u32[]{:S(2)}) %all-to-all-start.2) | async-done | bytes 557088 | tf_op jit(solution)/shard_map/all_to_all | solution.py:707
  137.8 1.0 relay.1.refs_9_
  138.8 3.5 %all-to-all-start.3 = ((bf16[8,128,256]{2,1,0:T(8,128)(2,1)}), bf16[8,128,256]{2,1,0:T(8,128)(2,1)S(1)}, u32[]{:S(2)}, u32[]{:S(2)}) async-start(bf16[8,128,256]{2,1,0:T(8,128)(2,1)} %relay.1.refs_9_), calls=%async_computation.3 | async-start | bytes 1048576 | tf_op jit(solution)/shard_map/all_to_all | solution.py:707
  142.3 6.6 %block_chunk.7 = (f32[2,256,1024]{2,1,0:T(8,128)}, bf16[2,256,1024]{2,1,0:T(8,128)(2,1)}, bf16[2,256,256]{2,1,0:T(8,128)(2,1)}, f32[2,8,128]{2,1,0:T(8,128)}) custom-call(bf16[8,580,256]{2,1,0:T(8,128)(2,1)} %copy-done, bf16[8,580,256]{2,1,0:T(8,128)(2,1)} %join.1.recv.refs_0_, f32[2,1280,4]{2,1,0:T(8,128)} %bitcast.13, ...), custom_call_target="tpu_custom_call" | custom-call | flops 4000000000 | bytes 10000000 | tf_op jit(solution)/shard_map/block_chunk/pallas_call | solution.py:553
  148.9 3.1 %all-to-all-done.3.refs_12_ = bf16[8,128,256]{2,1,0:T(8,128)(2,1)S(1)} async-done(((bf16[8,128,256]{2,1,0:T(8,128)(2,1)}), bf16[8,128,256]{2,1,0:T(8,128)(2,1)S(1)}, u32[]{:S(2)}, u32[]{:S(2)}) %all-to-all-start.3) | async-done | bytes 524320 | tf_op jit(solution)/shard_map/all_to_all | solution.py:707
  151.9 8.5 %finish.1 = bf16[1024,2048]{1,0:T(8,128)(2,1)} custom-call(f32[2,256,1024]{2,1,0:T(8,128)} %get-tuple-element.57.refs_0_, f32[2,256,1024]{2,1,0:T(8,128)} %get-tuple-element.65.refs_1_, f32[2,256,1024]{2,1,0:T(8,128)} %get-tuple-element.80.refs_2_, f32[2,256,1024]{2,1,0:T(8,128)} %get-tuple-element.90.refs_3_, ...), custom_call_target="tpu_custom_call" | custom-call | tf_op jit(solution)/shard_map/finish/pallas_call | solution.py:681
  (25 shorter events, 1.6 us)
Async XLA Ops:
  5.1 62.3 %all-to-all-start = ((bf16[8,592,512]{2,1,0:T(8,128)(2,1)}), bf16[8,592,512]{2,1,0:T(8,128)(2,1)}, u32[]{:S(2)}, u32[]{:S(2)}) async-start(bf16[8,592,512]{2,1,0:T(8,128)(2,1)} %cut_first.1.refs_0_), calls=%async_computation | async-start | bytes 9699328 | tf_op jit(solution)/shard_map/all_to_all | solution.py:707
  10.3 6.6 %copy-start.5 = (f32[4,2,1280]{2,1,0:T(2,128)S(1)}, f32[4,2,1280]{2,1,0:T(2,128)}, u32[]{:S(2)}) copy-start(f32[4,2,1280]{2,1,0:T(2,128)} %param.7) | copy-start | bytes 122884
  10.3 8.1 %copy-start.6 = (f32[32]{0:T(128)S(1)}, f32[32]{0:T(128)}, u32[]{:S(2)}) copy-start(f32[32]{0:T(128)} %param.8) | copy-start | bytes 388
  10.3 8.8 %copy-start.7 = (f32[32]{0:T(128)S(1)}, f32[32]{0:T(128)}, u32[]{:S(2)}) copy-start(f32[32]{0:T(128)} %param.9) | copy-start | bytes 388
  10.3 9.5 %copy-start.8 = (f32[32]{0:T(128)S(1)}, f32[32]{0:T(128)}, u32[]{:S(2)}) copy-start(f32[32]{0:T(128)} %param.10) | copy-start | bytes 388
  12.9 76.4 %collective-permute-start.1 = (bf16[580,512]{1,0:T(8,128)(2,1)}, bf16[580,512]{1,0:T(8,128)(2,1)S(1)}, u32[]{:S(2)}, u32[]{:S(2)}) collective-permute-start(bf16[580,512]{1,0:T(8,128)(2,1)} %get-tuple-element.68), channel_id=1, source_target_pairs={{0,8},{4,12},{8,0},{12,4},{16,24},{20,28},{24,16},{28,20},{1,9},{5... | collective-permute-start | bytes 1781768 | tf_op jit(solution)/shard_map/ppermute | solution.py:703
  15.3 74.0 %collective-permute-start.2 = (bf16[580,512]{1,0:T(8,128)(2,1)}, bf16[580,512]{1,0:T(8,128)(2,1)}, u32[]{:S(2)}, u32[]{:S(2)}) collective-permute-start(bf16[580,512]{1,0:T(8,128)(2,1)} %get-tuple-element.69), channel_id=1, source_target_pairs={{0,16},{4,20},{8,24},{12,28},{16,0},{20,4},{24,8},{28,12},{1,17},{... | collective-permute-start | bytes 1781768 | tf_op jit(solution)/shard_map/ppermute | solution.py:703
  16.8 76.2 %collective-permute-start.3 = (bf16[580,512]{1,0:T(8,128)(2,1)}, bf16[580,512]{1,0:T(8,128)(2,1)}, u32[]{:S(2)}, u32[]{:S(2)}) collective-permute-start(bf16[580,512]{1,0:T(8,128)(2,1)} %get-tuple-element.70), channel_id=1, source_target_pairs={{0,24},{4,28},{8,16},{12,20},{16,8},{20,12},{24,0},{28,4},{1,25},{... | collective-permute-start | bytes 1781768 | tf_op jit(solution)/shard_map/ppermute | solution.py:703
  67.4 50.4 %all-to-all-start.1 = ((bf16[8,580,256]{2,1,0:T(8,128)(2,1)}), bf16[8,580,256]{2,1,0:T(8,128)(2,1)S(1)}, u32[]{:S(2)}, u32[]{:S(2)}) async-start(bf16[8,580,256]{2,1,0:T(8,128)(2,1)} %cut_block.1), calls=%async_computation.1 | async-start | bytes 4784128 | tf_op jit(solution)/shard_map/all_to_all | solution.py:707
  89.3 3.7 %copy-start.2 = (bf16[580,512]{1,0:T(8,128)(2,1)}, bf16[580,512]{1,0:T(8,128)(2,1)S(1)}, u32[]{:S(2)}) copy-start(bf16[580,512]{1,0:T(8,128)(2,1)S(1)} %collective-permute-done.1.refs_0_) | copy-start | bytes 1781764
  95.0 7.2 %collective-permute-start.4 = (bf16[580,768]{1,0:T(8,128)(2,1)}, bf16[580,768]{1,0:T(8,128)(2,1)S(1)}, u32[]{:S(2)}, u32[]{:S(2)}) collective-permute-start(bf16[580,768]{1,0:T(8,128)(2,1)} %forward.1), channel_id=1, source_target_pairs={{0,4},{4,0},{8,12},{12,8},{16,20},{20,16},{24,28},{28,24},{1,5},{5... | collective-permute-start | bytes 2672648 | tf_op jit(solution)/shard_map/ppermute | solution.py:703
  95.0 7.1 %collective-permute-start = (bf16[580,256]{1,0:T(8,128)(2,1)}, bf16[580,256]{1,0:T(8,128)(2,1)S(1)}, u32[]{:S(2)}, u32[]{:S(2)}) collective-permute-start(bf16[580,256]{1,0:T(8,128)(2,1)} %get-tuple-element.67), channel_id=1, source_target_pairs={{0,4},{4,0},{8,12},{12,8},{16,20},{20,16},{24,28},{28,24},{1,5},{5... | collective-permute-start | bytes 890888 | tf_op jit(solution)/shard_map/ppermute | solution.py:703
  102.1 0.7 copy-start.4
  102.2 1.1 copy-start.3
  117.8 6.4 %copy-start = (bf16[8,580,256]{2,1,0:T(8,128)(2,1)}, bf16[8,580,256]{2,1,0:T(8,128)(2,1)S(1)}, u32[]{:S(2)}) copy-start(bf16[8,580,256]{2,1,0:T(8,128)(2,1)S(1)} %all-to-all-done.1.recv) | copy-start | bytes 7127044
  124.2 13.6 %all-to-all-start.2 = ((bf16[8,272,128]{2,1,0:T(8,128)(2,1)}), bf16[8,272,128]{2,1,0:T(8,128)(2,1)S(1)}, u32[]{:S(2)}, u32[]{:S(2)}) async-start(bf16[8,272,128]{2,1,0:T(8,128)(2,1)} %get-tuple-element.88), calls=%async_computation.2 | async-start | bytes 1114112 | tf_op jit(solution)/shard_map/all_to_all | solution.py:707
  138.8 13.2 %all-to-all-start.3 = ((bf16[8,128,256]{2,1,0:T(8,128)(2,1)}), bf16[8,128,256]{2,1,0:T(8,128)(2,1)S(1)}, u32[]{:S(2)}, u32[]{:S(2)}) async-start(bf16[8,128,256]{2,1,0:T(8,128)(2,1)} %relay.1.refs_9_), calls=%async_computation.3 | async-start | bytes 1048576 | tf_op jit(solution)/shard_map/all_to_all | solution.py:707
  142.3 9.7 %copy-start.1 = (f32[2048]{0:T(1024)S(1)}, f32[2048]{0:T(1024)}, u32[]{:S(2)}) copy-start(f32[2048]{0:T(1024)} %param.11) | copy-start | bytes 24580
where the time goes:
time: 161 us
  Pallas kernels  74.5 us (46%)
  waiting for transfers between devices  58.8 us (37%)
  starting transfers between devices  20.5 us (13%)
  local copies, waits for them, and re-layouts  6.38 us (4%)
    all_to_all x4, waiting for transfers between devices, exchange(): return lax.all_to_all(array, 'seq', split_axis=0, concat_axis=0, tiled=True)  55.1 us
    pallas_call x4, Pallas kernels, block_chunk(): pl.pallas_call(functools.partial(block_kernel, dims, chunk == 0), grid=(g...  26 us
    pallas_call x4, Pallas kernels, state_chunk(): pl.pallas_call(functools.partial(state_kernel, dims, chunk == 0, last), g...  24.4 us
    all_to_all x4, starting transfers between devices, exchange(): return lax.all_to_all(array, 'seq', split_axis=0, concat_axis=0, tiled=True)  16 us
    pallas_call x1, Pallas kernels, finish(): pl.pallas_call(functools.partial(final_kernel, chunks, groups), in_specs=...  8.49 us
    pallas_call x1, Pallas kernels, cut_first(): pl.pallas_call(first_kernel, in_specs=[anywhere], out_specs=anywhere, out...  5.07 us
    ppermute x5, starting transfers between devices, swap(): return lax.ppermute(array, 'seq', [(i, i ^ k) for i in range(count)])  4.52 us
    ppermute x5, waiting for transfers between devices, swap(): return lax.ppermute(array, 'seq', [(i, i ^ k) for i in range(count)])  3.74 us
  transfers between devices with their start and end apart: 9, of which 5 were waited for; matrix products, arithmetic and copies ran while one was open for 3% of the time, Pallas kernels for 33%

commit v1 on v0

--- a/solution.py
+++ b/solution.py
@@ -88,8 +88,8 @@
 
     for d in range(count):
         fetch(d).start()
-        if d:
-            window(d).start()
+    for d in range(1, count):
+        window(d).start()
     row = lax.broadcasted_iota(jnp.int32, (height, LANES), 0) - (rows - base)
     col = lax.broadcasted_iota(jnp.int32, (height, LANES), 1)
     hit = (row >= 0) & (col == lax.rem(row + 16, RIM) + LANES - RIM)
@@ -98,6 +98,7 @@
     for d in range(count):
         fetch(d).wait()
         place(d).start()
+    for d in range(count):
         end = held[d, base:rows, :].astype(f32)
         end = jnp.concatenate([end, jnp.zeros((height - end.shape[0], width), f32)], axis=0)
         if d:
@@ -606,7 +607,7 @@
 def final_kernel(chunks, groups, *refs):
     mixed, gates, sides = (refs[i * chunks : (i + 1) * chunks] for i in range(3))
     state, gain, out = refs[3 * chunks : 3 * chunks + 3]
-    held, gate_held, side_held, kept, carried, done, sems, out_sems = refs[3 * chunks + 3 :]
+    held, gate_held, side_held, kept, done, sems, out_sems = refs[3 * chunks + 3 :]
     span = held.shape[2]
     piece = state.shape[2]
     spg = state.shape[0] // groups
@@ -645,22 +646,26 @@
         if i >= 2:
             store(i - 2).wait()
         side = side_held[slot]
-        reach = jnp.dot(side[:, STATE_WIDTH:], spread, preferred_element_type=f32)
-        for j in range(spg):
-            lanes = slice(j * piece, (j + 1) * piece)
-            part = jnp.dot(
-                side[:, :STATE_WIDTH], state[g * spg + j], preferred_element_type=f32
-            )
-            carried[:, lanes] = part * reach[:, lanes]
-        for q in range(0, BLOCK, HEAD_DIM):
-            rows = slice(q, q + HEAD_DIM)
-            total = jnp.zeros((HEAD_DIM, LANES), f32)
-            for at in range(0, span, LANES):
-                lanes = slice(at, at + LANES)
-                gate = silu(gate_held[slot, rows, lanes].astype(f32))
-                v = held[slot, rows, lanes] + gate * carried[rows, lanes]
-                kept[rows, lanes] = v
-                total = total + v * v
+        half = BLOCK // 2
+        for q in range(0, BLOCK, half):
+            rows = slice(q, q + half)
+            total = jnp.zeros((half, LANES), f32)
+            for j in range(spg):
+                piece_lanes = slice(j * piece, (j + 1) * piece)
+                part = jnp.dot(
+                    side[rows, :STATE_WIDTH], state[g * spg + j], preferred_element_type=f32
+                )
+                reach = jnp.dot(
+                    side[rows, STATE_WIDTH:], spread[:, piece_lanes], preferred_element_type=f32
+                )
+                gate = silu(gate_held[slot, rows, piece_lanes].astype(f32))
+                v = held[slot, rows, piece_lanes] + gate * (part * reach)
+                kept[rows, piece_lanes] = v
+                for at in range(0, piece, LANES):
+                    t = v[:, at : at + LANES]
+                    if piece < LANES:
+                        t = jnp.concatenate([t, jnp.zeros((half, LANES - piece), f32)], axis=1)
+                    total = total + t * t
             mean = jnp.sum(total, axis=1, keepdims=True) * (1.0 / span)
             factor = lax.rsqrt(mean + EPSILON)
             for at in range(0, span, LANES):
@@ -687,7 +692,6 @@
             pltpu.VMEM((steps, BLOCK, span), f32),
             pltpu.VMEM((steps, BLOCK, span), bf16),
             pltpu.VMEM((steps, BLOCK, 2 * STATE_WIDTH), bf16),
-            pltpu.VMEM((BLOCK, span), f32),
             pltpu.VMEM((BLOCK, span), f32),
             pltpu.VMEM((2, BLOCK, span), bf16),
             pltpu.SemaphoreType.DMA((steps, 3)),

time: 161 us -> 162 us (level)
  no operation moved by 1% of the time
where the time goes in v1:
time: 162 us; the launch traced here: 161 us
  Pallas kernels  75.2 us (46%)
  waiting for transfers between devices  58.8 us (36%)
  starting transfers between devices  20.5 us (13%)
  local copies, waits for them, and re-layouts  6.38 us (4%)
    all_to_all x4, waiting for transfers between devices, exchange(): return lax.all_to_all(array, 'seq', split_axis=0, concat_axis=0, tiled=True)  55.1 us
    pallas_call x4, Pallas kernels, block_chunk(): pl.pallas_call(functools.partial(block_kernel, dims, chunk == 0), grid=(g...  26 us
    pallas_call x4, Pallas kernels, state_chunk(): pl.pallas_call(functools.partial(state_kernel, dims, chunk == 0, last), g...  24.4 us
    all_to_all x4, starting transfers between devices, exchange(): return lax.all_to_all(array, 'seq', split_axis=0, concat_axis=0, tiled=True)  16 us
    pallas_call x1, Pallas kernels, finish(): pl.pallas_call(functools.partial(final_kernel, chunks, groups), in_specs=...  8.26 us
    pallas_call x1, Pallas kernels, cut_first(): pl.pallas_call(first_kernel, in_specs=[anywhere], out_specs=anywhere, out...  6.01 us
    ppermute x5, starting transfers between devices, swap(): return lax.ppermute(array, 'seq', [(i, i ^ k) for i in range(count)])  4.52 us
    ppermute x5, waiting for transfers between devices, swap(): return lax.ppermute(array, 'seq', [(i, i ^ k) for i in range(count)])  3.73 us
  transfers between devices with their start and end apart: 9, of which 5 were waited for; matrix products, arithmetic and copies ran while one was open for 3% of the time, Pallas kernels for 33%

profile of v1, /device:TPU:0, one launch (start us, length us, event | category | flops | bytes accessed | tf_op | source)
XLA Modules:
  0.0 161.3 jit_solution(5776929334471314383)
XLA Ops:
  0.0 6.0 %cut_first.1.refs_0_ = bf16[8,592,512]{2,1,0:T(8,128)(2,1)} custom-call(bf16[580,8192]{1,0:T(8,128)(2,1)} %src.5), custom_call_target="tpu_custom_call" | custom-call | tf_op jit(solution)/shard_map/cut_first/pallas_call | solution.py:125
  6.0 5.2 %all-to-all-start = ((bf16[8,592,512]{2,1,0:T(8,128)(2,1)}), bf16[8,592,512]{2,1,0:T(8,128)(2,1)}, u32[]{:S(2)}, u32[]{:S(2)}) async-start(bf16[8,592,512]{2,1,0:T(8,128)(2,1)} %cut_first.1.refs_0_), calls=%async_computation | async-start | bytes 9699328 | tf_op jit(solution)/shard_map/all_to_all | solution.py:711
  11.2 2.6 %cut_pairs.1 = (bf16[580,256]{1,0:T(8,128)(2,1)}, bf16[580,256]{1,0:T(8,128)(2,1)}, bf16[580,512]{1,0:T(8,128)(2,1)}, bf16[580,512]{1,0:T(8,128)(2,1)}, bf16[580,512]{1,0:T(8,128)(2,1)}) custom-call(s32[1]{0:T(128)} %bitcast.1.me_ref, bf16[580,8192]{1,0:T(8,128)(2,1)} %src.5, bf16[8,592,512]{2,1,0:T(8,128)(2,1)} %cut_first.1.refs_0_), custom_call_target="tpu_custom_call" | custom-call | tf_op jit(solution)/shard_map/cut_pairs/pallas_call | solution.py:202
  13.8 2.4 %collective-permute-start.1 = (bf16[580,512]{1,0:T(8,128)(2,1)}, bf16[580,512]{1,0:T(8,128)(2,1)S(1)}, u32[]{:S(2)}, u32[]{:S(2)}) collective-permute-start(bf16[580,512]{1,0:T(8,128)(2,1)} %get-tuple-element.68), channel_id=1, source_target_pairs={{0,8},{4,12},{8,0},{12,4},{16,24},{20,28},{24,16},{28,20},{1,9},{5... | collective-permute-start | bytes 1781768 | tf_op jit(solution)/shard_map/ppermute | solution.py:707
  16.3 1.5 collective-permute-start.2
  17.8 1.5 copy.7
  19.3 0.7 reshape.20.refs_2_
  20.0 0.7 reshape.21.refs_3_
  20.7 0.7 reshape.22.refs_8_.refs_4_
  21.4 1.0 broadcast_in_dim.6.refs_4_.refs_7_.refs_6_
  23.1 2.5 %cut_block.1 = bf16[8,580,256]{2,1,0:T(8,128)(2,1)} custom-call(bf16[580,8192]{1,0:T(8,128)(2,1)} %src.5, bf16[580,256]{1,0:T(8,128)(2,1)} %get-tuple-element.66.own.refs_0_, f32[2,1280,4]{2,1,0:T(8,128)} %bitcast.5, f32[2,16,1]{2,1,0:T(8,128)} %reshape.20.refs_2_, f32[2,16,1]{2,1,0:T(8,128)} %reshape.21.refs_3_, f32[2,16,1]{2,1,0:T(8,128)} %reshape.22.refs_8_.refs_4_, ...), custom_call_target="tpu_custom_call" | custom-call | tf_op jit(solution)/shard_map/cut_block/pallas_call | solution.py:173
  25.6 42.7 %all-to-all-done.recv.refs_0_ = bf16[8,592,512]{2,1,0:T(8,128)(2,1)} async-done(((bf16[8,592,512]{2,1,0:T(8,128)(2,1)}), bf16[8,592,512]{2,1,0:T(8,128)(2,1)}, u32[]{:S(2)}, u32[]{:S(2)}) %all-to-all-start) | async-done | bytes 4849696 | tf_op jit(solution)/shard_map/all_to_all | solution.py:711
  68.3 3.6 %all-to-all-start.1 = ((bf16[8,580,256]{2,1,0:T(8,128)(2,1)}), bf16[8,580,256]{2,1,0:T(8,128)(2,1)S(1)}, u32[]{:S(2)}, u32[]{:S(2)}) async-start(bf16[8,580,256]{2,1,0:T(8,128)(2,1)} %cut_block.1), calls=%async_computation.1 | async-start | bytes 4784128 | tf_op jit(solution)/shard_map/all_to_all | solution.py:711
  71.9 6.1 %state_chunk.4 = (bf16[2,1024,256]{2,1,0:T(8,128)(2,1)}, bf16[2,128,256]{2,1,0:T(8,128)(2,1)}, f32[2,16,256]{2,1,0:T(8,128)}, f32[2,16,256]{2,1,0:T(8,128)}, f32...) custom-call(bf16[8,592,512]{2,1,0:T(8,128)(2,1)} %all-to-all-done.recv.refs_0_, ...), custom_call_target="tpu_custom_call" | custom-call | flops 4000000000 | bytes 10000000 | tf_op jit(solution)/shard_map/state_chunk/pallas_call | solution.py:423
  78.0 6.0 %state_chunk.5 = (bf16[2,1024,256]{2,1,0:T(8,128)(2,1)}, bf16[2,128,256]{2,1,0:T(8,128)(2,1)}, f32[2,16,256]{2,1,0:T(8,128)}, f32[2,16,256]{2,1,0:T(8,128)}, f32...) custom-call(bf16[8,592,512]{2,1,0:T(8,128)(2,1)} %all-to-all-done.recv.refs_0_, ...), custom_call_target="tpu_custom_call" | custom-call | flops 4000000000 | bytes 10000000 | tf_op jit(solution)/shard_map/state_chunk/pallas_call | solution.py:423
  84.0 6.2 %block_chunk.4 = (f32[2,256,1024]{2,1,0:T(8,128)}, bf16[2,256,1024]{2,1,0:T(8,128)(2,1)}, bf16[2,256,256]{2,1,0:T(8,128)(2,1)}, f32[2,8,128]{2,1,0:T(8,128)}) custom-call(bf16[8,592,512]{2,1,0:T(8,128)(2,1)} %all-to-all-done.recv.refs_0_, bf16[8,592,512]{2,1,0:T(8,128)(2,1)} %all-to-all-done.recv.refs_0_, f32[2,1280,4]{2,1,0:T(8,128)} %bitcast.8, ...), custom_call_target="tpu_custom_call" | custom-call | flops 4000000000 | bytes 10000000 | tf_op jit(solution)/shard_map/block_chunk/pallas_call | solution.py:554
  90.2 3.7 %collective-permute-done.3.refs_2_ = bf16[580,512]{1,0:T(8,128)(2,1)} collective-permute-done((bf16[580,512]{1,0:T(8,128)(2,1)}, bf16[580,512]{1,0:T(8,128)(2,1)}, u32[]{:S(2)}, u32[]{:S(2)}) %collective-permute-start.3) | collective-permute-done | bytes 593952 | tf_op jit(solution)/shard_map/ppermute | solution.py:707
  94.0 1.9 %forward.1 = bf16[580,768]{1,0:T(8,128)(2,1)} custom-call(bf16[580,512]{1,0:T(8,128)(2,1)} %copy-done.2, bf16[580,512]{1,0:T(8,128)(2,1)} %collective-permute-done.2.refs_1_, bf16[580,512]{1,0:T(8,128)(2,1)} %collective-permute-done.3.refs_2_, f32[2,16,128]{2,1,0:T(8,128)} %get-tuple-element.71.refs_3_.refs_5_, f32[2,8,128]{2,1,0:T(8,128)} %get-tuple-element.72.refs_4_), custom_call_target="tpu_custom_call" | custom-call | tf_op jit(solution)/shard_map/forward/pallas_call | solution.py:226
  96.5 6.6 %block_chunk.5 = (f32[2,256,1024]{2,1,0:T(8,128)}, bf16[2,256,1024]{2,1,0:T(8,128)(2,1)}, bf16[2,256,256]{2,1,0:T(8,128)(2,1)}, f32[2,8,128]{2,1,0:T(8,128)}) custom-call(bf16[8,592,512]{2,1,0:T(8,128)(2,1)} %all-to-all-done.recv.refs_0_, bf16[8,592,512]{2,1,0:T(8,128)(2,1)} %all-to-all-done.recv.refs_0_, f32[2,1280,4]{2,1,0:T(8,128)} %bitcast.9, ...), custom_call_target="tpu_custom_call" | custom-call | flops 4000000000 | bytes 10000000 | tf_op jit(solution)/shard_map/block_chunk/pallas_call | solution.py:554
  103.1 0.7 copy-done.4
  104.2 2.5 %join.1.recv.refs_0_ = bf16[8,580,256]{2,1,0:T(8,128)(2,1)} custom-call(s32[1]{0:T(128)} %bitcast.1.me_ref, bf16[580,256]{1,0:T(8,128)(2,1)} %get-tuple-element.66.own.refs_0_, bf16[580,256]{1,0:T(8,128)(2,1)} %copy-done.4, bf16[580,512]{1,0:T(8,128)(2,1)} %copy-done.2, bf16[580,512]{1,0:T(8,128)(2,1)} %collective-permute-done.2.refs_1_, ...), custom_call_target="tpu_custom_call" | custom-call | tf_op jit(solution)/shard_map/join/pallas_call | solution.py:252
  106.7 6.0 %state_chunk.6 = (bf16[2,1024,256]{2,1,0:T(8,128)(2,1)}, bf16[2,128,256]{2,1,0:T(8,128)(2,1)}, f32[2,16,256]{2,1,0:T(8,128)}, f32[2,16,256]{2,1,0:T(8,128)}, f32...) custom-call(bf16[8,580,256]{2,1,0:T(8,128)(2,1)} %join.1.recv.refs_0_, ...), custom_call_target="tpu_custom_call" | custom-call | flops 4000000000 | bytes 10000000 | tf_op jit(solution)/shard_map/state_chunk/pallas_call | solution.py:423
  112.6 6.1 %all-to-all-done.1.recv = bf16[8,580,256]{2,1,0:T(8,128)(2,1)S(1)} async-done(((bf16[8,580,256]{2,1,0:T(8,128)(2,1)}), bf16[8,580,256]{2,1,0:T(8,128)(2,1)S(1)}, u32[]{:S(2)}, u32[]{:S(2)}) %all-to-all-start.1) | async-done | bytes 2375712 | tf_op jit(solution)/shard_map/all_to_all | solution.py:711
  118.7 6.4 %state_chunk.7 = (bf16[2,1024,256]{2,1,0:T(8,128)(2,1)}, bf16[2,128,256]{2,1,0:T(8,128)(2,1)}, f32[2,16,256]{2,1,0:T(8,128)}, f32[2,16,256]{2,1,0:T(8,128)}, f32...) custom-call(bf16[8,580,256]{2,1,0:T(8,128)(2,1)S(1)} %all-to-all-done.1.recv, ...), custom_call_target="tpu_custom_call" | custom-call | flops 4000000000 | bytes 10000000 | tf_op jit(solution)/shard_map/state_chunk/pallas_call | solution.py:423
  125.1 3.7 %all-to-all-start.2 = ((bf16[8,272,128]{2,1,0:T(8,128)(2,1)}), bf16[8,272,128]{2,1,0:T(8,128)(2,1)S(1)}, u32[]{:S(2)}, u32[]{:S(2)}) async-start(bf16[8,272,128]{2,1,0:T(8,128)(2,1)} %get-tuple-element.88), calls=%async_computation.2 | async-start | bytes 1114112 | tf_op jit(solution)/shard_map/all_to_all | solution.py:711
  128.9 6.6 %block_chunk.6 = (f32[2,256,1024]{2,1,0:T(8,128)}, bf16[2,256,1024]{2,1,0:T(8,128)(2,1)}, bf16[2,256,256]{2,1,0:T(8,128)(2,1)}, f32[2,8,128]{2,1,0:T(8,128)}) custom-call(bf16[8,580,256]{2,1,0:T(8,128)(2,1)} %join.1.recv.refs_0_, bf16[8,592,512]{2,1,0:T(8,128)(2,1)} %all-to-all-done.recv.refs_0_, f32[2,1280,4]{2,1,0:T(8,128)} %bitcast.12, ...), custom_call_target="tpu_custom_call" | custom-call | flops 4000000000 | bytes 10000000 | tf_op jit(solution)/shard_map/block_chunk/pallas_call | solution.py:554
  135.5 3.2 %all-to-all-done.2.src = bf16[8,272,128]{2,1,0:T(8,128)(2,1)S(1)} async-done(((bf16[8,272,128]{2,1,0:T(8,128)(2,1)}), bf16[8,272,128]{2,1,0:T(8,128)(2,1)S(1)}, u32[]{:S(2)}, u32[]{:S(2)}) %all-to-all-start.2) | async-done | bytes 557088 | tf_op jit(solution)/shard_map/all_to_all | solution.py:711
  138.7 1.0 relay.1.refs_9_
  139.7 3.5 %all-to-all-start.3 = ((bf16[8,128,256]{2,1,0:T(8,128)(2,1)}), bf16[8,128,256]{2,1,0:T(8,128)(2,1)S(1)}, u32[]{:S(2)}, u32[]{:S(2)}) async-start(bf16[8,128,256]{2,1,0:T(8,128)(2,1)} %relay.1.refs_9_), calls=%async_computation.3 | async-start | bytes 1048576 | tf_op jit(solution)/shard_map/all_to_all | solution.py:711
  143.2 6.6 %block_chunk.7 = (f32[2,256,1024]{2,1,0:T(8,128)}, bf16[2,256,1024]{2,1,0:T(8,128)(2,1)}, bf16[2,256,256]{2,1,0:T(8,128)(2,1)}, f32[2,8,128]{2,1,0:T(8,128)}) custom-call(bf16[8,580,256]{2,1,0:T(8,128)(2,1)} %copy-done, bf16[8,580,256]{2,1,0:T(8,128)(2,1)} %join.1.recv.refs_0_, f32[2,1280,4]{2,1,0:T(8,128)} %bitcast.13, ...), custom_call_target="tpu_custom_call" | custom-call | flops 4000000000 | bytes 10000000 | tf_op jit(solution)/shard_map/block_chunk/pallas_call | solution.py:554
  149.8 3.1 %all-to-all-done.3.refs_12_ = bf16[8,128,256]{2,1,0:T(8,128)(2,1)S(1)} async-done(((bf16[8,128,256]{2,1,0:T(8,128)(2,1)}), bf16[8,128,256]{2,1,0:T(8,128)(2,1)S(1)}, u32[]{:S(2)}, u32[]{:S(2)}) %all-to-all-start.3) | async-done | bytes 524320 | tf_op jit(solution)/shard_map/all_to_all | solution.py:711
  152.9 8.3 %finish.1 = bf16[1024,2048]{1,0:T(8,128)(2,1)} custom-call(f32[2,256,1024]{2,1,0:T(8,128)} %get-tuple-element.57.refs_0_, f32[2,256,1024]{2,1,0:T(8,128)} %get-tuple-element.65.refs_1_, f32[2,256,1024]{2,1,0:T(8,128)} %get-tuple-element.80.refs_2_, f32[2,256,1024]{2,1,0:T(8,128)} %get-tuple-element.90.refs_3_, ...), custom_call_target="tpu_custom_call" | custom-call | tf_op jit(solution)/shard_map/finish/pallas_call | solution.py:686
  (25 shorter events, 1.6 us)
Async XLA Ops:
  6.0 62.3 %all-to-all-start = ((bf16[8,592,512]{2,1,0:T(8,128)(2,1)}), bf16[8,592,512]{2,1,0:T(8,128)(2,1)}, u32[]{:S(2)}, u32[]{:S(2)}) async-start(bf16[8,592,512]{2,1,0:T(8,128)(2,1)} %cut_first.1.refs_0_), calls=%async_computation | async-start | bytes 9699328 | tf_op jit(solution)/shard_map/all_to_all | solution.py:711
  11.2 6.6 %copy-start.5 = (f32[4,2,1280]{2,1,0:T(2,128)S(1)}, f32[4,2,1280]{2,1,0:T(2,128)}, u32[]{:S(2)}) copy-start(f32[4,2,1280]{2,1,0:T(2,128)} %param.7) | copy-start | bytes 122884
  11.2 8.1 %copy-start.6 = (f32[32]{0:T(128)S(1)}, f32[32]{0:T(128)}, u32[]{:S(2)}) copy-start(f32[32]{0:T(128)} %param.8) | copy-start | bytes 388
  11.2 8.8 %copy-start.7 = (f32[32]{0:T(128)S(1)}, f32[32]{0:T(128)}, u32[]{:S(2)}) copy-start(f32[32]{0:T(128)} %param.9) | copy-start | bytes 388
  11.2 9.5 %copy-start.8 = (f32[32]{0:T(128)S(1)}, f32[32]{0:T(128)}, u32[]{:S(2)}) copy-start(f32[32]{0:T(128)} %param.10) | copy-start | bytes 388
  13.8 76.4 %collective-permute-start.1 = (bf16[580,512]{1,0:T(8,128)(2,1)}, bf16[580,512]{1,0:T(8,128)(2,1)S(1)}, u32[]{:S(2)}, u32[]{:S(2)}) collective-permute-start(bf16[580,512]{1,0:T(8,128)(2,1)} %get-tuple-element.68), channel_id=1, source_target_pairs={{0,8},{4,12},{8,0},{12,4},{16,24},{20,28},{24,16},{28,20},{1,9},{5... | collective-permute-start | bytes 1781768 | tf_op jit(solution)/shard_map/ppermute | solution.py:707
  16.3 74.0 %collective-permute-start.2 = (bf16[580,512]{1,0:T(8,128)(2,1)}, bf16[580,512]{1,0:T(8,128)(2,1)}, u32[]{:S(2)}, u32[]{:S(2)}) collective-permute-start(bf16[580,512]{1,0:T(8,128)(2,1)} %get-tuple-element.69), channel_id=1, source_target_pairs={{0,16},{4,20},{8,24},{12,28},{16,0},{20,4},{24,8},{28,12},{1,17},{... | collective-permute-start | bytes 1781768 | tf_op jit(solution)/shard_map/ppermute | solution.py:707
  17.8 76.2 %collective-permute-start.3 = (bf16[580,512]{1,0:T(8,128)(2,1)}, bf16[580,512]{1,0:T(8,128)(2,1)}, u32[]{:S(2)}, u32[]{:S(2)}) collective-permute-start(bf16[580,512]{1,0:T(8,128)(2,1)} %get-tuple-element.70), channel_id=1, source_target_pairs={{0,24},{4,28},{8,16},{12,20},{16,8},{20,12},{24,0},{28,4},{1,25},{... | collective-permute-start | bytes 1781768 | tf_op jit(solution)/shard_map/ppermute | solution.py:707
  68.3 50.4 %all-to-all-start.1 = ((bf16[8,580,256]{2,1,0:T(8,128)(2,1)}), bf16[8,580,256]{2,1,0:T(8,128)(2,1)S(1)}, u32[]{:S(2)}, u32[]{:S(2)}) async-start(bf16[8,580,256]{2,1,0:T(8,128)(2,1)} %cut_block.1), calls=%async_computation.1 | async-start | bytes 4784128 | tf_op jit(solution)/shard_map/all_to_all | solution.py:711
  90.2 3.7 %copy-start.2 = (bf16[580,512]{1,0:T(8,128)(2,1)}, bf16[580,512]{1,0:T(8,128)(2,1)S(1)}, u32[]{:S(2)}) copy-start(bf16[580,512]{1,0:T(8,128)(2,1)S(1)} %collective-permute-done.1.refs_0_) | copy-start | bytes 1781764
  95.9 7.2 %collective-permute-start.4 = (bf16[580,768]{1,0:T(8,128)(2,1)}, bf16[580,768]{1,0:T(8,128)(2,1)S(1)}, u32[]{:S(2)}, u32[]{:S(2)}) collective-permute-start(bf16[580,768]{1,0:T(8,128)(2,1)} %forward.1), channel_id=1, source_target_pairs={{0,4},{4,0},{8,12},{12,8},{16,20},{20,16},{24,28},{28,24},{1,5},{5... | collective-permute-start | bytes 2672648 | tf_op jit(solution)/shard_map/ppermute | solution.py:707
  96.0 7.1 %collective-permute-start = (bf16[580,256]{1,0:T(8,128)(2,1)}, bf16[580,256]{1,0:T(8,128)(2,1)S(1)}, u32[]{:S(2)}, u32[]{:S(2)}) collective-permute-start(bf16[580,256]{1,0:T(8,128)(2,1)} %get-tuple-element.67), channel_id=1, source_target_pairs={{0,4},{4,0},{8,12},{12,8},{16,20},{20,16},{24,28},{28,24},{1,5},{5... | collective-permute-start | bytes 890888 | tf_op jit(solution)/shard_map/ppermute | solution.py:707
  103.1 0.7 copy-start.4
  103.1 1.1 copy-start.3
  118.7 6.4 %copy-start = (bf16[8,580,256]{2,1,0:T(8,128)(2,1)}, bf16[8,580,256]{2,1,0:T(8,128)(2,1)S(1)}, u32[]{:S(2)}) copy-start(bf16[8,580,256]{2,1,0:T(8,128)(2,1)S(1)} %all-to-all-done.1.recv) | copy-start | bytes 7127044
  125.1 13.6 %all-to-all-start.2 = ((bf16[8,272,128]{2,1,0:T(8,128)(2,1)}), bf16[8,272,128]{2,1,0:T(8,128)(2,1)S(1)}, u32[]{:S(2)}, u32[]{:S(2)}) async-start(bf16[8,272,128]{2,1,0:T(8,128)(2,1)} %get-tuple-element.88), calls=%async_computation.2 | async-start | bytes 1114112 | tf_op jit(solution)/shard_map/all_to_all | solution.py:711
  139.7 13.2 %all-to-all-start.3 = ((bf16[8,128,256]{2,1,0:T(8,128)(2,1)}), bf16[8,128,256]{2,1,0:T(8,128)(2,1)S(1)}, u32[]{:S(2)}, u32[]{:S(2)}) async-start(bf16[8,128,256]{2,1,0:T(8,128)(2,1)} %relay.1.refs_9_), calls=%async_computation.3 | async-start | bytes 1048576 | tf_op jit(solution)/shard_map/all_to_all | solution.py:711
  143.2 9.7 %copy-start.1 = (f32[2048]{0:T(1024)S(1)}, f32[2048]{0:T(1024)}, u32[]{:S(2)}) copy-start(f32[2048]{0:T(1024)} %param.11) | copy-start | bytes 24580

commit v2 on v1

--- a/solution.py
+++ b/solution.py
@@ -88,8 +88,8 @@
 
     for d in range(count):
         fetch(d).start()
-    for d in range(1, count):
-        window(d).start()
+        if d:
+            window(d).start()
     row = lax.broadcasted_iota(jnp.int32, (height, LANES), 0) - (rows - base)
     col = lax.broadcasted_iota(jnp.int32, (height, LANES), 1)
     hit = (row >= 0) & (col == lax.rem(row + 16, RIM) + LANES - RIM)
@@ -98,7 +98,6 @@
     for d in range(count):
         fetch(d).wait()
         place(d).start()
-    for d in range(count):
         end = held[d, base:rows, :].astype(f32)
         end = jnp.concatenate([end, jnp.zeros((height - end.shape[0], width), f32)], axis=0)
         if d:
@@ -471,7 +470,7 @@
     spg, rows, heads, span, piece_heads = dims
     prev, refs = refs[0], refs[1:]
     w, xact, bmap, run_ref, dt_ref, cum_ref, state, skip = refs[:8]
-    mixed, gate_out, side, token, raw, low, shifted = refs[-7:]
+    mixed, passed, c_out, token, raw, low, shifted = refs[-7:]
     at_c = 2 * span + STATE_WIDTH
     gather_rows(recv, prev, first, raw, rows, at_c, at_c + STATE_WIDTH, True, at_c // rows)
     gather_rows(recv, prev, first, raw, rows, 0, span, False)
@@ -492,10 +491,8 @@
     if not first:
         cc = jnp.concatenate([c, c], axis=0)
         entered = jnp.exp2(r)
-    reach = [part.astype(f32) for part in split(jnp.exp(cum_ref[0]))]
-    reach.append(jnp.zeros((STATE_WIDTH - 2 * heads, BLOCK), f32))
-    side[0, :, :STATE_WIDTH] = c.astype(f32).T.astype(bf16)
-    side[0, :, STATE_WIDTH:] = jnp.concatenate(reach, axis=0).T.astype(bf16)
+    reach = jnp.exp(cum_ref[0])
+    c_out[0] = c.astype(f32).T.astype(bf16)
     turned = []
     for h in range(heads):
         at = h * HEAD_DIM
@@ -513,13 +510,13 @@
                 both = jnp.concatenate(split(state[0, at : at + WIDE, :]), axis=1)
                 carried = jnp.dot(both, cc, preferred_element_type=f32)
             y = y + entered[h : h + 1, :] * carried[at % WIDE : at % WIDE + HEAD_DIM, :]
-        gate = raw[at : at + HEAD_DIM, LANES:]
-        turned.append((y * silu(gate), gate))
+        gate = silu(raw[at : at + HEAD_DIM, LANES:])
+        turned.append((y * gate, gate * reach[h : h + 1, :]))
         if len(turned) * HEAD_DIM == LANES:
             lanes = slice(at + HEAD_DIM - LANES, at + HEAD_DIM)
             mixed[0, :, lanes] = jnp.concatenate([pair[0] for pair in turned], axis=0).T
             wide = jnp.concatenate([pair[1] for pair in turned], axis=0).T
-            gate_out[0, :, lanes] = wide.astype(bf16)
+            passed[0, :, lanes] = wide.astype(bf16)
             turned = []
 
 
@@ -558,13 +555,13 @@
         out_specs=[
             per_group(BLOCK, span),
             per_group(BLOCK, span),
-            per_group(BLOCK, 2 * STATE_WIDTH),
+            per_group(BLOCK, STATE_WIDTH),
             per_group(8, LANES),
         ],
         out_shape=[
             out(f32, BLOCK, span),
             out(bf16, BLOCK, span),
-            out(bf16, BLOCK, 2 * STATE_WIDTH),
+            out(bf16, BLOCK, STATE_WIDTH),
             out(f32, 8, LANES),
         ],
         scratch_shapes=[
@@ -605,25 +602,24 @@
 
 
 def final_kernel(chunks, groups, *refs):
-    mixed, gates, sides = (refs[i * chunks : (i + 1) * chunks] for i in range(3))
-    state, gain, out = refs[3 * chunks : 3 * chunks + 3]
-    held, gate_held, side_held, kept, done, sems, out_sems = refs[3 * chunks + 3 :]
-    span = held.shape[2]
+    mixed, passed, maps = (refs[i * chunks : (i + 1) * chunks] for i in range(3))
+    state_src, gain_src, out = refs[3 * chunks : 3 * chunks + 3]
+    held, passed_held, map_held, state, gain, kept, done = refs[3 * chunks + 3 : -3]
+    sems, few_sems, out_sems = refs[-3:]
+    span = kept.shape[1]
     piece = state.shape[2]
     spg = state.shape[0] // groups
-    heads = span // HEAD_DIM
+    half = BLOCK // 2
     steps = [(g, c) for g in range(groups) for c in range(chunks)]
 
     def loads(i):
         g, c = steps[i]
-        slot = i
-        moves = []
-        moves.append((sides[c].at[g], side_held.at[slot]))
-        moves.append((mixed[c].at[g], held.at[slot]))
-        moves.append((gates[c].at[g], gate_held.at[slot]))
-        return [
-            pltpu.make_async_copy(a, b, sems.at[slot, j]) for j, (a, b) in enumerate(moves)
+        moves = [
+            (maps[c].at[g], map_held.at[i]),
+            (mixed[c].at[g], held.at[i]),
+            (passed[c].at[g], passed_held.at[i]),
         ]
+        return [pltpu.make_async_copy(a, b, sems.at[i, j]) for j, (a, b) in enumerate(moves)]
 
     def store(i):
         g, c = steps[i]
@@ -633,33 +629,32 @@
             out_sems.at[i % 2],
         )
 
+    few = [
+        pltpu.make_async_copy(state_src, state, few_sems.at[0]),
+        pltpu.make_async_copy(gain_src, gain, few_sems.at[1]),
+    ]
+    for move in few:
+        move.start()
     for i in range(len(steps)):
         for move in loads(i):
             move.start()
-    row = lax.broadcasted_iota(jnp.int32, (STATE_WIDTH, span), 0)
-    col = lax.broadcasted_iota(jnp.int32, (STATE_WIDTH, span), 1) // HEAD_DIM
-    spread = jnp.where((row == col) | (row == col + heads), 1.0, 0.0).astype(bf16)
+    for move in few:
+        move.wait()
     for i, (g, c) in enumerate(steps):
-        slot = i
         for move in loads(i):
             move.wait()
         if i >= 2:
             store(i - 2).wait()
-        side = side_held[slot]
-        half = BLOCK // 2
         for q in range(0, BLOCK, half):
             rows = slice(q, q + half)
             total = jnp.zeros((half, LANES), f32)
             for j in range(spg):
                 piece_lanes = slice(j * piece, (j + 1) * piece)
-                part = jnp.dot(
-                    side[rows, :STATE_WIDTH], state[g * spg + j], preferred_element_type=f32
+                carried = jnp.dot(
+                    map_held[i, rows, :], state[g * spg + j], preferred_element_type=f32
                 )
-                reach = jnp.dot(
-                    side[rows, STATE_WIDTH:], spread[:, piece_lanes], preferred_element_type=f32
-                )
-                gate = silu(gate_held[slot, rows, piece_lanes].astype(f32))
-                v = held[slot, rows, piece_lanes] + gate * (part * reach)
+                scale = passed_held[i, rows, piece_lanes].astype(f32)
+                v = held[i, rows, piece_lanes] + scale * carried
                 kept[rows, piece_lanes] = v
                 for at in range(0, piece, LANES):
                     t = v[:, at : at + LANES]
@@ -677,29 +672,31 @@
         store(i).wait()
 
 
-def finish(mixed, gates, sides, state, gain):
+def finish(mixed, passed, maps, state, gain):
     chunks = len(mixed)
     groups, _, span = mixed[0].shape
     steps = groups * chunks
     anywhere = pl.BlockSpec(memory_space=pl.ANY)
-    within = pl.BlockSpec(memory_space=pltpu.VMEM)
     return pl.pallas_call(
         functools.partial(final_kernel, chunks, groups),
-        in_specs=[anywhere] * (3 * chunks) + [within] * 2,
+        in_specs=[anywhere] * (3 * chunks + 2),
         out_specs=anywhere,
         out_shape=jax.ShapeDtypeStruct((chunks * BLOCK, groups * span), bf16),
         scratch_shapes=[
             pltpu.VMEM((steps, BLOCK, span), f32),
             pltpu.VMEM((steps, BLOCK, span), bf16),
-            pltpu.VMEM((steps, BLOCK, 2 * STATE_WIDTH), bf16),
+            pltpu.VMEM((steps, BLOCK, STATE_WIDTH), bf16),
+            pltpu.VMEM(state.shape, bf16),
+            pltpu.VMEM(gain.shape, f32),
             pltpu.VMEM((BLOCK, span), f32),
             pltpu.VMEM((2, BLOCK, span), bf16),
             pltpu.SemaphoreType.DMA((steps, 3)),
             pltpu.SemaphoreType.DMA((2,)),
+            pltpu.SemaphoreType.DMA((2,)),
         ],
         compiler_params=params(40),
         name="finish",
-    )(*in_hbm(*mixed, *gates, *sides), state, gain)
+    )(*in_hbm(*mixed, *passed, *maps), state, gain)
 
 
 def swap(array, k):

time: 162 us -> 160 us (0.988)
  Pallas kernels: 75.2 us -> 73.2 us
  transfers between devices with their start and end apart: 9 -> 9, of which waited for: 5 -> 5; matrix products, arithmetic and copies ran while one was open for 3% -> 3% of each run, Pallas kernels for 33% -> 34%
where the time goes in v2:
time: 160 us; the launch traced here: 159 us
  Pallas kernels  73.2 us (46%)
  waiting for transfers between devices  58.9 us (37%)
  starting transfers between devices  20.6 us (13%)
  local copies, waits for them, and re-layouts  6.32 us (4%)
    all_to_all x4, waiting for transfers between devices, exchange(): return lax.all_to_all(array, 'seq', split_axis=0, concat_axis=0, tiled=True)  55.2 us
    pallas_call x4, Pallas kernels, block_chunk(): pl.pallas_call(functools.partial(block_kernel, dims, chunk == 0), grid=(g...  26 us
    pallas_call x4, Pallas kernels, state_chunk(): pl.pallas_call(functools.partial(state_kernel, dims, chunk == 0, last), g...  24.4 us
    all_to_all x4, starting transfers between devices, exchange(): return lax.all_to_all(array, 'seq', split_axis=0, concat_axis=0, tiled=True)  16 us
    pallas_call x1, Pallas kernels, finish(): pl.pallas_call(functools.partial(final_kernel, chunks, groups), in_specs=...  7.2 us
    pallas_call x1, Pallas kernels, cut_first(): pl.pallas_call(first_kernel, in_specs=[anywhere], out_specs=anywhere, out...  5.08 us
    ppermute x5, starting transfers between devices, swap(): return lax.ppermute(array, 'seq', [(i, i ^ k) for i in range(count)])  4.53 us
    ppermute x5, waiting for transfers between devices, swap(): return lax.ppermute(array, 'seq', [(i, i ^ k) for i in range(count)])  3.71 us
  transfers between devices with their start and end apart: 9, of which 5 were waited for; matrix products, arithmetic and copies ran while one was open for 3% of the time, Pallas kernels for 34%

profile of v2, /device:TPU:0, one launch (start us, length us, event | category | flops | bytes accessed | tf_op | source)
XLA Modules:
  0.0 159.3 jit_solution(1895570399316878015)
XLA Ops:
  0.0 5.1 %cut_first.1.refs_0_ = bf16[8,592,512]{2,1,0:T(8,128)(2,1)} custom-call(bf16[580,8192]{1,0:T(8,128)(2,1)} %src.5), custom_call_target="tpu_custom_call" | custom-call | tf_op jit(solution)/shard_map/cut_first/pallas_call | solution.py:124
  5.1 5.2 %all-to-all-start = ((bf16[8,592,512]{2,1,0:T(8,128)(2,1)}), bf16[8,592,512]{2,1,0:T(8,128)(2,1)}, u32[]{:S(2)}, u32[]{:S(2)}) async-start(bf16[8,592,512]{2,1,0:T(8,128)(2,1)} %cut_first.1.refs_0_), calls=%async_computation | async-start | bytes 9699328 | tf_op jit(solution)/shard_map/all_to_all | solution.py:708
  10.3 2.6 %cut_pairs.1 = (bf16[580,256]{1,0:T(8,128)(2,1)}, bf16[580,256]{1,0:T(8,128)(2,1)}, bf16[580,512]{1,0:T(8,128)(2,1)}, bf16[580,512]{1,0:T(8,128)(2,1)}, bf16[580,512]{1,0:T(8,128)(2,1)}) custom-call(s32[1]{0:T(128)} %bitcast.1.me_ref, bf16[580,8192]{1,0:T(8,128)(2,1)} %src.5, bf16[8,592,512]{2,1,0:T(8,128)(2,1)} %cut_first.1.refs_0_), custom_call_target="tpu_custom_call" | custom-call | tf_op jit(solution)/shard_map/cut_pairs/pallas_call | solution.py:201
  12.9 2.4 %collective-permute-start.1 = (bf16[580,512]{1,0:T(8,128)(2,1)}, bf16[580,512]{1,0:T(8,128)(2,1)S(1)}, u32[]{:S(2)}, u32[]{:S(2)}) collective-permute-start(bf16[580,512]{1,0:T(8,128)(2,1)} %get-tuple-element.68), channel_id=1, source_target_pairs={{0,8},{4,12},{8,0},{12,4},{16,24},{20,28},{24,16},{28,20},{1,9},{5... | collective-permute-start | bytes 1781768 | tf_op jit(solution)/shard_map/ppermute | solution.py:704
  15.3 1.6 collective-permute-start.2
  16.9 1.5 copy.7
  18.4 0.7 reshape.20.refs_2_
  19.1 0.7 reshape.21.refs_3_
  19.8 0.7 reshape.22.refs_8_.refs_4_
  20.5 1.0 broadcast_in_dim.6.refs_4_.refs_7_.refs_6_
  22.2 2.5 %cut_block.1 = bf16[8,580,256]{2,1,0:T(8,128)(2,1)} custom-call(bf16[580,8192]{1,0:T(8,128)(2,1)} %src.5, bf16[580,256]{1,0:T(8,128)(2,1)} %get-tuple-element.66.own.refs_0_, f32[2,1280,4]{2,1,0:T(8,128)} %bitcast.5, f32[2,16,1]{2,1,0:T(8,128)} %reshape.20.refs_2_, f32[2,16,1]{2,1,0:T(8,128)} %reshape.21.refs_3_, f32[2,16,1]{2,1,0:T(8,128)} %reshape.22.refs_8_.refs_4_, ...), custom_call_target="tpu_custom_call" | custom-call | tf_op jit(solution)/shard_map/cut_block/pallas_call | solution.py:172
  24.7 42.7 %all-to-all-done.recv.refs_0_ = bf16[8,592,512]{2,1,0:T(8,128)(2,1)} async-done(((bf16[8,592,512]{2,1,0:T(8,128)(2,1)}), bf16[8,592,512]{2,1,0:T(8,128)(2,1)}, u32[]{:S(2)}, u32[]{:S(2)}) %all-to-all-start) | async-done | bytes 4849696 | tf_op jit(solution)/shard_map/all_to_all | solution.py:708
  67.4 3.6 %all-to-all-start.1 = ((bf16[8,580,256]{2,1,0:T(8,128)(2,1)}), bf16[8,580,256]{2,1,0:T(8,128)(2,1)S(1)}, u32[]{:S(2)}, u32[]{:S(2)}) async-start(bf16[8,580,256]{2,1,0:T(8,128)(2,1)} %cut_block.1), calls=%async_computation.1 | async-start | bytes 4784128 | tf_op jit(solution)/shard_map/all_to_all | solution.py:708
  71.0 6.1 %state_chunk.4 = (bf16[2,1024,256]{2,1,0:T(8,128)(2,1)}, bf16[2,128,256]{2,1,0:T(8,128)(2,1)}, f32[2,16,256]{2,1,0:T(8,128)}, f32[2,16,256]{2,1,0:T(8,128)}, f32...) custom-call(bf16[8,592,512]{2,1,0:T(8,128)(2,1)} %all-to-all-done.recv.refs_0_, ...), custom_call_target="tpu_custom_call" | custom-call | flops 4000000000 | bytes 10000000 | tf_op jit(solution)/shard_map/state_chunk/pallas_call | solution.py:422
  77.1 6.0 %state_chunk.5 = (bf16[2,1024,256]{2,1,0:T(8,128)(2,1)}, bf16[2,128,256]{2,1,0:T(8,128)(2,1)}, f32[2,16,256]{2,1,0:T(8,128)}, f32[2,16,256]{2,1,0:T(8,128)}, f32...) custom-call(bf16[8,592,512]{2,1,0:T(8,128)(2,1)} %all-to-all-done.recv.refs_0_, ...), custom_call_target="tpu_custom_call" | custom-call | flops 4000000000 | bytes 10000000 | tf_op jit(solution)/shard_map/state_chunk/pallas_call | solution.py:422
  83.0 6.3 %block_chunk.4 = (f32[2,256,1024]{2,1,0:T(8,128)}, bf16[2,256,1024]{2,1,0:T(8,128)(2,1)}, bf16[2,256,128]{2,1,0:T(8,128)(2,1)}, f32[2,8,128]{2,1,0:T(8,128)}) custom-call(bf16[8,592,512]{2,1,0:T(8,128)(2,1)} %all-to-all-done.recv.refs_0_, bf16[8,592,512]{2,1,0:T(8,128)(2,1)} %all-to-all-done.recv.refs_0_, f32[2,1280,4]{2,1,0:T(8,128)} %bitcast.8, ...), custom_call_target="tpu_custom_call" | custom-call | flops 4000000000 | bytes 10000000 | tf_op jit(solution)/shard_map/block_chunk/pallas_call | solution.py:551
  89.4 3.7 %collective-permute-done.3.refs_2_ = bf16[580,512]{1,0:T(8,128)(2,1)} collective-permute-done((bf16[580,512]{1,0:T(8,128)(2,1)}, bf16[580,512]{1,0:T(8,128)(2,1)}, u32[]{:S(2)}, u32[]{:S(2)}) %collective-permute-start.3) | collective-permute-done | bytes 593952 | tf_op jit(solution)/shard_map/ppermute | solution.py:704
  93.1 1.9 %forward.1 = bf16[580,768]{1,0:T(8,128)(2,1)} custom-call(bf16[580,512]{1,0:T(8,128)(2,1)} %copy-done.2, bf16[580,512]{1,0:T(8,128)(2,1)} %collective-permute-done.2.refs_1_, bf16[580,512]{1,0:T(8,128)(2,1)} %collective-permute-done.3.refs_2_, f32[2,16,128]{2,1,0:T(8,128)} %get-tuple-element.71.refs_3_.refs_5_, f32[2,8,128]{2,1,0:T(8,128)} %get-tuple-element.72.refs_4_), custom_call_target="tpu_custom_call" | custom-call | tf_op jit(solution)/shard_map/forward/pallas_call | solution.py:225
  95.6 6.6 %block_chunk.5 = (f32[2,256,1024]{2,1,0:T(8,128)}, bf16[2,256,1024]{2,1,0:T(8,128)(2,1)}, bf16[2,256,128]{2,1,0:T(8,128)(2,1)}, f32[2,8,128]{2,1,0:T(8,128)}) custom-call(bf16[8,592,512]{2,1,0:T(8,128)(2,1)} %all-to-all-done.recv.refs_0_, bf16[8,592,512]{2,1,0:T(8,128)(2,1)} %all-to-all-done.recv.refs_0_, f32[2,1280,4]{2,1,0:T(8,128)} %bitcast.9, ...), custom_call_target="tpu_custom_call" | custom-call | flops 4000000000 | bytes 10000000 | tf_op jit(solution)/shard_map/block_chunk/pallas_call | solution.py:551
  102.3 0.7 copy-done.4
  103.3 2.5 %join.1.recv.refs_0_ = bf16[8,580,256]{2,1,0:T(8,128)(2,1)} custom-call(s32[1]{0:T(128)} %bitcast.1.me_ref, bf16[580,256]{1,0:T(8,128)(2,1)} %get-tuple-element.66.own.refs_0_, bf16[580,256]{1,0:T(8,128)(2,1)} %copy-done.4, bf16[580,512]{1,0:T(8,128)(2,1)} %copy-done.2, bf16[580,512]{1,0:T(8,128)(2,1)} %collective-permute-done.2.refs_1_, ...), custom_call_target="tpu_custom_call" | custom-call | tf_op jit(solution)/shard_map/join/pallas_call | solution.py:251
  105.8 6.0 %state_chunk.6 = (bf16[2,1024,256]{2,1,0:T(8,128)(2,1)}, bf16[2,128,256]{2,1,0:T(8,128)(2,1)}, f32[2,16,256]{2,1,0:T(8,128)}, f32[2,16,256]{2,1,0:T(8,128)}, f32...) custom-call(bf16[8,580,256]{2,1,0:T(8,128)(2,1)} %join.1.recv.refs_0_, ...), custom_call_target="tpu_custom_call" | custom-call | flops 4000000000 | bytes 10000000 | tf_op jit(solution)/shard_map/state_chunk/pallas_call | solution.py:422
  111.7 6.1 %all-to-all-done.1.recv = bf16[8,580,256]{2,1,0:T(8,128)(2,1)S(1)} async-done(((bf16[8,580,256]{2,1,0:T(8,128)(2,1)}), bf16[8,580,256]{2,1,0:T(8,128)(2,1)S(1)}, u32[]{:S(2)}, u32[]{:S(2)}) %all-to-all-start.1) | async-done | bytes 2375712 | tf_op jit(solution)/shard_map/all_to_all | solution.py:708
  117.8 6.4 %state_chunk.7 = (bf16[2,1024,256]{2,1,0:T(8,128)(2,1)}, bf16[2,128,256]{2,1,0:T(8,128)(2,1)}, f32[2,16,256]{2,1,0:T(8,128)}, f32[2,16,256]{2,1,0:T(8,128)}, f32...) custom-call(bf16[8,580,256]{2,1,0:T(8,128)(2,1)S(1)} %all-to-all-done.1.recv, ...), custom_call_target="tpu_custom_call" | custom-call | flops 4000000000 | bytes 10000000 | tf_op jit(solution)/shard_map/state_chunk/pallas_call | solution.py:422
  124.2 3.7 %all-to-all-start.2 = ((bf16[8,272,128]{2,1,0:T(8,128)(2,1)}), bf16[8,272,128]{2,1,0:T(8,128)(2,1)S(1)}, u32[]{:S(2)}, u32[]{:S(2)}) async-start(bf16[8,272,128]{2,1,0:T(8,128)(2,1)} %get-tuple-element.88), calls=%async_computation.2 | async-start | bytes 1114112 | tf_op jit(solution)/shard_map/all_to_all | solution.py:708
  127.9 6.6 %block_chunk.6 = (f32[2,256,1024]{2,1,0:T(8,128)}, bf16[2,256,1024]{2,1,0:T(8,128)(2,1)}, bf16[2,256,128]{2,1,0:T(8,128)(2,1)}, f32[2,8,128]{2,1,0:T(8,128)}) custom-call(bf16[8,580,256]{2,1,0:T(8,128)(2,1)} %join.1.recv.refs_0_, bf16[8,592,512]{2,1,0:T(8,128)(2,1)} %all-to-all-done.recv.refs_0_, f32[2,1280,4]{2,1,0:T(8,128)} %bitcast.12, ...), custom_call_target="tpu_custom_call" | custom-call | flops 4000000000 | bytes 10000000 | tf_op jit(solution)/shard_map/block_chunk/pallas_call | solution.py:551
  134.5 3.3 %all-to-all-done.2.src = bf16[8,272,128]{2,1,0:T(8,128)(2,1)S(1)} async-done(((bf16[8,272,128]{2,1,0:T(8,128)(2,1)}), bf16[8,272,128]{2,1,0:T(8,128)(2,1)S(1)}, u32[]{:S(2)}, u32[]{:S(2)}) %all-to-all-start.2) | async-done | bytes 557088 | tf_op jit(solution)/shard_map/all_to_all | solution.py:708
  137.8 1.0 relay.1.refs_9_
  138.8 3.5 %all-to-all-start.3 = ((bf16[8,128,256]{2,1,0:T(8,128)(2,1)}), bf16[8,128,256]{2,1,0:T(8,128)(2,1)S(1)}, u32[]{:S(2)}, u32[]{:S(2)}) async-start(bf16[8,128,256]{2,1,0:T(8,128)(2,1)} %relay.1.refs_9_), calls=%async_computation.3 | async-start | bytes 1048576 | tf_op jit(solution)/shard_map/all_to_all | solution.py:708
  142.3 6.5 %block_chunk.7 = (f32[2,256,1024]{2,1,0:T(8,128)}, bf16[2,256,1024]{2,1,0:T(8,128)(2,1)}, bf16[2,256,128]{2,1,0:T(8,128)(2,1)}, f32[2,8,128]{2,1,0:T(8,128)}) custom-call(bf16[8,580,256]{2,1,0:T(8,128)(2,1)} %copy-done, bf16[8,580,256]{2,1,0:T(8,128)(2,1)} %join.1.recv.refs_0_, f32[2,1280,4]{2,1,0:T(8,128)} %bitcast.13, ...), custom_call_target="tpu_custom_call" | custom-call | flops 4000000000 | bytes 10000000 | tf_op jit(solution)/shard_map/block_chunk/pallas_call | solution.py:551
  148.8 3.1 %all-to-all-done.3.refs_12_ = bf16[8,128,256]{2,1,0:T(8,128)(2,1)S(1)} async-done(((bf16[8,128,256]{2,1,0:T(8,128)(2,1)}), bf16[8,128,256]{2,1,0:T(8,128)(2,1)S(1)}, u32[]{:S(2)}, u32[]{:S(2)}) %all-to-all-start.3) | async-done | bytes 524320 | tf_op jit(solution)/shard_map/all_to_all | solution.py:708
  152.0 7.2 %finish.1 = bf16[1024,2048]{1,0:T(8,128)(2,1)} custom-call(f32[2,256,1024]{2,1,0:T(8,128)} %get-tuple-element.57.refs_0_, f32[2,256,1024]{2,1,0:T(8,128)} %get-tuple-element.65.refs_1_, f32[2,256,1024]{2,1,0:T(8,128)} %get-tuple-element.80.refs_2_, f32[2,256,1024]{2,1,0:T(8,128)} %get-tuple-element.90.refs_3_, ...), custom_call_target="tpu_custom_call" | custom-call | tf_op jit(solution)/shard_map/finish/pallas_call | solution.py:680
  (25 shorter events, 1.5 us)
Async XLA Ops:
  5.1 62.3 %all-to-all-start = ((bf16[8,592,512]{2,1,0:T(8,128)(2,1)}), bf16[8,592,512]{2,1,0:T(8,128)(2,1)}, u32[]{:S(2)}, u32[]{:S(2)}) async-start(bf16[8,592,512]{2,1,0:T(8,128)(2,1)} %cut_first.1.refs_0_), calls=%async_computation | async-start | bytes 9699328 | tf_op jit(solution)/shard_map/all_to_all | solution.py:708
  10.3 6.6 %copy-start.5 = (f32[4,2,1280]{2,1,0:T(2,128)S(1)}, f32[4,2,1280]{2,1,0:T(2,128)}, u32[]{:S(2)}) copy-start(f32[4,2,1280]{2,1,0:T(2,128)} %param.7) | copy-start | bytes 122884
  10.3 8.1 %copy-start.6 = (f32[32]{0:T(128)S(1)}, f32[32]{0:T(128)}, u32[]{:S(2)}) copy-start(f32[32]{0:T(128)} %param.8) | copy-start | bytes 388
  10.3 8.8 %copy-start.7 = (f32[32]{0:T(128)S(1)}, f32[32]{0:T(128)}, u32[]{:S(2)}) copy-start(f32[32]{0:T(128)} %param.9) | copy-start | bytes 388
  10.3 9.5 %copy-start.8 = (f32[32]{0:T(128)S(1)}, f32[32]{0:T(128)}, u32[]{:S(2)}) copy-start(f32[32]{0:T(128)} %param.10) | copy-start | bytes 388
  12.9 76.4 %collective-permute-start.1 = (bf16[580,512]{1,0:T(8,128)(2,1)}, bf16[580,512]{1,0:T(8,128)(2,1)S(1)}, u32[]{:S(2)}, u32[]{:S(2)}) collective-permute-start(bf16[580,512]{1,0:T(8,128)(2,1)} %get-tuple-element.68), channel_id=1, source_target_pairs={{0,8},{4,12},{8,0},{12,4},{16,24},{20,28},{24,16},{28,20},{1,9},{5... | collective-permute-start | bytes 1781768 | tf_op jit(solution)/shard_map/ppermute | solution.py:704
  15.3 74.1 %collective-permute-start.2 = (bf16[580,512]{1,0:T(8,128)(2,1)}, bf16[580,512]{1,0:T(8,128)(2,1)}, u32[]{:S(2)}, u32[]{:S(2)}) collective-permute-start(bf16[580,512]{1,0:T(8,128)(2,1)} %get-tuple-element.69), channel_id=1, source_target_pairs={{0,16},{4,20},{8,24},{12,28},{16,0},{20,4},{24,8},{28,12},{1,17},{... | collective-permute-start | bytes 1781768 | tf_op jit(solution)/shard_map/ppermute | solution.py:704
  16.9 76.2 %collective-permute-start.3 = (bf16[580,512]{1,0:T(8,128)(2,1)}, bf16[580,512]{1,0:T(8,128)(2,1)}, u32[]{:S(2)}, u32[]{:S(2)}) collective-permute-start(bf16[580,512]{1,0:T(8,128)(2,1)} %get-tuple-element.70), channel_id=1, source_target_pairs={{0,24},{4,28},{8,16},{12,20},{16,8},{20,12},{24,0},{28,4},{1,25},{... | collective-permute-start | bytes 1781768 | tf_op jit(solution)/shard_map/ppermute | solution.py:704
  67.4 50.4 %all-to-all-start.1 = ((bf16[8,580,256]{2,1,0:T(8,128)(2,1)}), bf16[8,580,256]{2,1,0:T(8,128)(2,1)S(1)}, u32[]{:S(2)}, u32[]{:S(2)}) async-start(bf16[8,580,256]{2,1,0:T(8,128)(2,1)} %cut_block.1), calls=%async_computation.1 | async-start | bytes 4784128 | tf_op jit(solution)/shard_map/all_to_all | solution.py:708
  89.4 3.7 %copy-start.2 = (bf16[580,512]{1,0:T(8,128)(2,1)}, bf16[580,512]{1,0:T(8,128)(2,1)S(1)}, u32[]{:S(2)}) copy-start(bf16[580,512]{1,0:T(8,128)(2,1)S(1)} %collective-permute-done.1.refs_0_) | copy-start | bytes 1781764
  95.0 7.2 %collective-permute-start.4 = (bf16[580,768]{1,0:T(8,128)(2,1)}, bf16[580,768]{1,0:T(8,128)(2,1)S(1)}, u32[]{:S(2)}, u32[]{:S(2)}) collective-permute-start(bf16[580,768]{1,0:T(8,128)(2,1)} %forward.1), channel_id=1, source_target_pairs={{0,4},{4,0},{8,12},{12,8},{16,20},{20,16},{24,28},{28,24},{1,5},{5... | collective-permute-start | bytes 2672648 | tf_op jit(solution)/shard_map/ppermute | solution.py:704
  95.1 7.1 %collective-permute-start = (bf16[580,256]{1,0:T(8,128)(2,1)}, bf16[580,256]{1,0:T(8,128)(2,1)S(1)}, u32[]{:S(2)}, u32[]{:S(2)}) collective-permute-start(bf16[580,256]{1,0:T(8,128)(2,1)} %get-tuple-element.67), channel_id=1, source_target_pairs={{0,4},{4,0},{8,12},{12,8},{16,20},{20,16},{24,28},{28,24},{1,5},{5... | collective-permute-start | bytes 890888 | tf_op jit(solution)/shard_map/ppermute | solution.py:704
  102.2 0.7 copy-start.4
  102.2 1.0 copy-start.3
  117.8 6.4 %copy-start = (bf16[8,580,256]{2,1,0:T(8,128)(2,1)}, bf16[8,580,256]{2,1,0:T(8,128)(2,1)S(1)}, u32[]{:S(2)}) copy-start(bf16[8,580,256]{2,1,0:T(8,128)(2,1)S(1)} %all-to-all-done.1.recv) | copy-start | bytes 7127044
  124.2 13.6 %all-to-all-start.2 = ((bf16[8,272,128]{2,1,0:T(8,128)(2,1)}), bf16[8,272,128]{2,1,0:T(8,128)(2,1)S(1)}, u32[]{:S(2)}, u32[]{:S(2)}) async-start(bf16[8,272,128]{2,1,0:T(8,128)(2,1)} %get-tuple-element.88), calls=%async_computation.2 | async-start | bytes 1114112 | tf_op jit(solution)/shard_map/all_to_all | solution.py:708
  138.8 13.2 %all-to-all-start.3 = ((bf16[8,128,256]{2,1,0:T(8,128)(2,1)}), bf16[8,128,256]{2,1,0:T(8,128)(2,1)S(1)}, u32[]{:S(2)}, u32[]{:S(2)}) async-start(bf16[8,128,256]{2,1,0:T(8,128)(2,1)} %relay.1.refs_9_), calls=%async_computation.3 | async-start | bytes 1048576 | tf_op jit(solution)/shard_map/all_to_all | solution.py:708
  142.3 9.7 %copy-start.1 = (f32[2048]{0:T(1024)S(1)}, f32[2048]{0:T(1024)}, u32[]{:S(2)}) copy-start(f32[2048]{0:T(1024)} %param.11) | copy-start | bytes 24580
